TPU v7x, 32 devices: a whole 2x2x4 slice. The times are simulated.
32 devices in a mesh: dp: 8 (over y, x, core), mp: 4 (over z).
Axes of the slice: x: 2, y: 2, z: 4, core: 2. Of those that a mesh axis runs over, the one named last changes fastest.
Arguments:
- video: bfloat16 [8, 8, 784, 768], P('mp', 'dp'), may hold values from -6 to 6
- patch_width: int32 [8], P('dp'), may hold values from 196 to 784, as said below
- temporal_gain: float32 [768], replicated, may hold values from 0.25 to 1.75
- temporal_shift: float32 [768], replicated, may hold values from -1.75 to 1.75
- temporal_qkv: bfloat16 [768, 2304], replicated, may hold values from -0.21875 to 0.21875
- temporal_qv_bias: float32 [1536], replicated, may hold values from -1.75 to 1.75
- temporal_proj: bfloat16 [768, 768], replicated, may hold values from -0.625 to 0.625
- temporal_proj_bias: float32 [768], replicated, may hold values from -1.75 to 1.75
- spatial_gain: float32 [768], replicated, may hold values from 0.25 to 1.75
- spatial_shift: float32 [768], replicated, may hold values from -1.75 to 1.75
- spatial_qkv: bfloat16 [768, 2304], replicated, may hold values from -0.21875 to 0.21875
- spatial_qv_bias: float32 [1536], replicated, may hold values from -1.75 to 1.75
- spatial_proj: bfloat16 [768, 768], replicated, may hold values from -2 to 2
- spatial_proj_bias: float32 [768], replicated, may hold values from -1.75 to 1.75
- mlp_gain: float32 [768], replicated, may hold values from 0.25 to 1.75
- mlp_shift: float32 [768], replicated, may hold values from -1.75 to 1.75
- fc1_weight: bfloat16 [768, 3072], P(None, 'mp'), may hold values from -0.21875 to 0.21875
- fc1_bias: bfloat16 [3072], P('mp'), may hold values from -1.75 to 1.75
- fc2_weight: bfloat16 [3072, 768], P('mp'), may hold values from -0.109375 to 0.109375
- fc2_bias: float32 [768], replicated, may hold values from -1.75 to 1.75
- cotangent: bfloat16 [8, 8, 784, 768], P('mp', 'dp'), may hold values from -6 to 6
Outputs:
- output: bfloat16 [8, 8, 784, 768], P('mp', 'dp')
- video_grad: float32 [8, 8, 784, 768], P('mp', 'dp')
- temporal_gain_grad: float32 [768], replicated
- temporal_shift_grad: float32 [768], replicated
- temporal_qkv_grad: float32 [768, 2304], replicated
- temporal_qv_bias_grad: float32 [1536], replicated
- temporal_proj_grad: float32 [768, 768], replicated
- temporal_proj_bias_grad: float32 [768], replicated
- spatial_gain_grad: float32 [768], replicated
- spatial_shift_grad: float32 [768], replicated
- spatial_qkv_grad: float32 [768, 2304], replicated
- spatial_qv_bias_grad: float32 [1536], replicated
- spatial_proj_grad: float32 [768, 768], replicated
- spatial_proj_bias_grad: float32 [768], replicated
- mlp_gain_grad: float32 [768], replicated
- mlp_shift_grad: float32 [768], replicated
- fc1_weight_grad: float32 [768, 3072], P('dp', 'mp')
- fc1_bias_grad: float32 [3072], replicated
- fc2_weight_grad: float32 [3072, 768], P('mp', 'dp')
- fc2_bias_grad: float32 [768], replicated
Inputs may be any that keep to these rules, and one draw needn't show every extreme that they name: `patch_width`: each set holds either one clip of 784 patches per frame or four clips of 196; sets of both kinds occur in every draw. Every clip has all 8 frames.
All inputs are finite; a program needn't handle non-finite values.
Results may differ from a plain program's by a relative error of at most 0.017.
Values may be sent and summed in bfloat16 or wider, within the bound.
A program may use at most 384 MiB of HBM per device.

v0:
```python
import functools
import jax
import jax.numpy as jnp
from jax import lax
from jax.experimental import pallas as pl
from jax.experimental.pallas import tpu as pltpu
from jax.sharding import PartitionSpec as P

HEADS = 12
HEAD_DIM = 64
GROUP = 4
WIDE = GROUP * HEAD_DIM
EPSILON = 1e-06
F32 = jnp.float32
BF16 = jnp.bfloat16
MIB = 1 << 20


def params(mib=56):
    return pltpu.CompilerParams(vmem_limit_bytes=mib * MIB)


def dot(a, b):
    return jnp.dot(a, b, preferred_element_type=F32)


def dot_nt(a, b):
    return lax.dot_general(a, b, (((1,), (1,)), ((), ())), preferred_element_type=F32)


def dot_tn(a, b):
    return lax.dot_general(a, b, (((0,), (0,)), ((), ())), preferred_element_type=F32)


def head_lanes(rows, head, dtype):
    lane = lax.broadcasted_iota(jnp.int32, (rows, WIDE), 1)
    return (lane // HEAD_DIM == head).astype(dtype)


def windows(slots, clips, rows):
    size = slots // clips
    found = []
    for start in range(0, slots, rows):
        stop = min(start + rows, slots)
        low = start // size * size // 16 * 16
        high = min(-(-(-(-stop // size) * size) // 16) * 16, slots)
        found.append((start, stop, low, high))
    return found


def spatial_fwd_body(width_ref, q_ref, k_ref, v_ref, o_ref, l_ref, *, slots, rows, narrow):
    def attend(chunks, size):
        stats = []
        for start, stop, low, high in chunks:
            count = stop - start
            q = q_ref[start:stop, :]
            k = k_ref[low:high, :]
            v = v_ref[low:high, :]
            if size < slots:
                query_clip = (lax.broadcasted_iota(jnp.int32, (count, high - low), 0) + start) // size
                key_clip = (lax.broadcasted_iota(jnp.int32, (count, high - low), 1) + low) // size
                same = query_clip == key_clip
            total = jnp.zeros((count, WIDE), F32)
            lse = jnp.zeros((count, 128), F32)
            lane = lax.broadcasted_iota(jnp.int32, (count, 128), 1)
            for head in range(GROUP):
                s = dot_nt(q * head_lanes(count, head, BF16), k)
                if size < slots:
                    s = jnp.where(same, s, -1e30)
                top = jnp.max(s, axis=1, keepdims=True)
                e = jnp.exp(s - top)
                norm = jnp.sum(e, axis=1, keepdims=True)
                o = dot(e.astype(BF16), v)
                total = total + o * (head_lanes(count, head, F32) / norm)
                lse = jnp.where(lane == head, top + jnp.log(norm), lse)
            o_ref[start:stop, :] = total.astype(BF16)
            stats.append(lse)
        l_ref[...] = jnp.concatenate(stats, axis=0).T[:8, :]

    wide = width_ref[0] == slots

    @pl.when(wide)
    def _():
        attend(windows(slots, 1, rows or slots), slots)

    @pl.when(jnp.logical_not(wide))
    def _():
        attend(windows(slots, 4, narrow), slots // 4)


def spatial_fwd(width, qkv, frames, slots, rows=None, narrow=256):
    groups = HEADS // GROUP
    qkv = qkv.reshape(frames, slots, -1)
    spec = lambda part: pl.BlockSpec((None, slots, WIDE), lambda f, g, w: (f, 0, part * groups + g))
    out = pl.pallas_call(
        functools.partial(spatial_fwd_body, slots=slots, rows=rows, narrow=narrow),
        grid_spec=pltpu.PrefetchScalarGridSpec(
            num_scalar_prefetch=1,
            grid=(frames, groups),
            in_specs=[spec(0), spec(1), spec(2)],
            out_specs=[
                pl.BlockSpec((None, slots, WIDE), lambda f, g, w: (f, 0, g)),
                pl.BlockSpec((None, None, 8, slots), lambda f, g, w: (f, g, 0, 0)),
            ],
        ),
        out_shape=[
            jax.ShapeDtypeStruct((frames, slots, HEADS * HEAD_DIM), BF16),
            jax.ShapeDtypeStruct((frames, groups, 8, slots), F32),
        ],
        cost_estimate=pl.CostEstimate(flops=20 * 10**9, bytes_accessed=5 * MIB, transcendentals=0),
        compiler_params=params(),
        name="spatial_fwd",
    )(width, qkv, qkv, qkv)
    return out


def spatial_bwd_body(width_ref, q_ref, k_ref, v_ref, o_ref, l_ref, g_ref, dq_ref, dk_ref, dv_ref, dqt, *, slots, rows, narrow):
    prod = g_ref[...].astype(F32) * o_ref[...].astype(F32)
    high_part = prod.astype(BF16)
    low_part = (prod - high_part.astype(F32)).astype(BF16)
    lane = lax.broadcasted_iota(jnp.int32, (8, WIDE), 1)
    row = lax.broadcasted_iota(jnp.int32, (8, WIDE), 0)
    picks = (lane // HEAD_DIM == row).astype(BF16)
    delta = dot_nt(picks, high_part) + dot_nt(picks, low_part)

    def attend(chunks, size):
        dqt[...] = jnp.zeros_like(dqt)
        kt = k_ref[...].T
        for start, stop, low, high in chunks:
            count = stop - start
            k = k_ref[start:stop, :]
            v = v_ref[start:stop, :]
            q = q_ref[low:high, :]
            g = g_ref[low:high, :]
            if size < slots:
                key_clip = (lax.broadcasted_iota(jnp.int32, (count, high - low), 0) + start) // size
                query_clip = (lax.broadcasted_iota(jnp.int32, (count, high - low), 1) + low) // size
                same = query_clip == key_clip
            dk = jnp.zeros((count, WIDE), F32)
            dv = jnp.zeros((count, WIDE), F32)
            for head in range(GROUP):
                mask = head_lanes(count, head, BF16)
                s = dot_nt(k * mask, q)
                p = jnp.exp(s - l_ref[head : head + 1, low:high])
                if size < slots:
                    p = jnp.where(same, p, 0.0)
                dp = dot_nt(v * mask, g)
                ds = (p * (dp - delta[head : head + 1, low:high])).astype(BF16)
                keep = head_lanes(count, head, F32)
                dv = dv + dot(p.astype(BF16), g) * keep
                dk = dk + dot(ds, q) * keep
                span = slice(head * HEAD_DIM, (head + 1) * HEAD_DIM)
                dqt[span, low:high] += dot(kt[span, start:stop], ds)
            dk_ref[start:stop, :] = dk.astype(BF16)
            dv_ref[start:stop, :] = dv.astype(BF16)
        dq_ref[...] = (dqt[...] * HEAD_DIM**-0.5).T.astype(BF16)

    wide = width_ref[0] == slots

    @pl.when(wide)
    def _():
        attend(windows(slots, 1, rows or slots), slots)

    @pl.when(jnp.logical_not(wide))
    def _():
        attend(windows(slots, 4, narrow), slots // 4)


def spatial_bwd(frame, width, qkv, mixed, lse, grad, frames, slots, rows=None, narrow=208):
    groups = HEADS // GROUP
    width_all = HEADS * HEAD_DIM
    qkv = qkv.reshape(frames, slots, -1)
    spec = lambda part: pl.BlockSpec((None, slots, WIDE), lambda f, g, w: (f, 0, part * groups + g))
    one = pl.BlockSpec((None, slots, WIDE), lambda f, g, w: (f, 0, g))
    out = pl.pallas_call(
        functools.partial(spatial_bwd_body, slots=slots, rows=rows, narrow=narrow),
        grid_spec=pltpu.PrefetchScalarGridSpec(
            num_scalar_prefetch=1,
            grid=(frames, groups),
            in_specs=[
                spec(0), spec(1), spec(2), one,
                pl.BlockSpec((None, None, 8, slots), lambda f, g, w: (f, g, 0, 0)),
                pl.BlockSpec((None, slots, WIDE), lambda f, g, w: (frame + f, 0, g)),
            ],
            out_specs=[one, one, one],
            scratch_shapes=[pltpu.VMEM((WIDE, slots), F32)],
        ),
        out_shape=[jax.ShapeDtypeStruct((frames, slots, width_all), BF16)] * 3,
        cost_estimate=pl.CostEstimate(flops=32 * 10**9, bytes_accessed=9 * MIB, transcendentals=0),
        compiler_params=params(),
        name="spatial_bwd",
    )(width, qkv, qkv, qkv, mixed, lse, grad)
    return out


def fixed(shape):
    return pl.BlockSpec(shape, lambda *_: (0,) * len(shape))


def norm_parts(value):
    centered = value - jnp.mean(value, axis=-1, keepdims=True)
    scale = lax.rsqrt(jnp.mean(centered * centered, axis=-1, keepdims=True) + EPSILON)
    return centered * scale, scale


def norm_grad(grad, unit, scale, gain):
    inner = grad * gain
    return scale * (
        inner
        - jnp.mean(inner, axis=-1, keepdims=True)
        - unit * jnp.mean(inner * unit, axis=-1, keepdims=True)
    )


def column_sum(value):
    return jnp.sum(value.astype(F32), axis=0, keepdims=True)


def by_part(parts, share, width):
    return pl.BlockSpec((parts, None, share, width), lambda f: (0, f, 0, 0))


def norm_in_body(video_ref, gain_ref, shift_ref, out_ref):
    unit, _ = norm_parts(video_ref[...].astype(F32))
    split_positions(out_ref, (unit * gain_ref[...] + shift_ref[...]).astype(BF16))


def split_positions(out_ref, value):
    parts, share, width = out_ref.shape
    slots = value.shape[0]
    for part in range(parts):
        start = part * share
        count = min(max(slots - start, 0), share)
        if count > 0:
            out_ref[part, :count, :] = value[start : start + count, :]
        if count < share:
            out_ref[part, count:, :] = jnp.zeros((share - count, width), value.dtype)


def joined_positions(ref, slots):
    parts, share, width = ref.shape
    return ref[...].reshape(parts * share, width)[:slots, :]


def norm_in(video, gain, shift, parts, share):
    frames, slots, width = video.shape
    return pl.pallas_call(
        norm_in_body,
        grid=(frames,),
        in_specs=[pl.BlockSpec((None, slots, width), lambda f: (f, 0, 0)), fixed((width,)), fixed((width,))],
        out_specs=by_part(parts, share, width),
        out_shape=jax.ShapeDtypeStruct((parts, frames, share, width), BF16),
        cost_estimate=pl.CostEstimate(flops=1 * 10**9, bytes_accessed=10 * MIB, transcendentals=0),
        compiler_params=params(),
        name="norm_in",
    )(video, gain, shift)


STEP = 16


def stacked(block, rows):
    return jnp.concatenate([block * head_lanes(rows, head, BF16) for head in range(GROUP)], axis=0)


def temporal_fwd_body(x_ref, wq_ref, wk_ref, wv_ref, bq_ref, bv_ref, q_ref, k_ref, v_ref, *o_refs):
    frames, slots, width = x_ref.shape
    x = x_ref[...].reshape(frames * slots, width)
    shape = (frames, slots, WIDE)
    q_ref[...] = ((dot(x, wq_ref[...]) + bq_ref[...]) * HEAD_DIM**-0.5).astype(BF16).reshape(shape)
    k_ref[...] = dot(x, wk_ref[...]).astype(BF16).reshape(shape)
    v_ref[...] = (dot(x, wv_ref[...]) + bv_ref[...]).astype(BF16).reshape(shape)
    rows = frames * STEP
    row = lax.broadcasted_iota(jnp.int32, (rows, rows), 0)
    col = lax.broadcasted_iota(jnp.int32, (rows, rows), 1)
    same = row % STEP == col % STEP
    for step in range(slots // STEP):
        part = slice(step * STEP, (step + 1) * STEP)
        q = q_ref[:, part, :].reshape(rows, WIDE)
        keys = stacked(k_ref[:, part, :].reshape(rows, WIDE), rows)
        values = stacked(v_ref[:, part, :].reshape(rows, WIDE), rows)
        scores = dot_nt(q, keys)
        mixing = []
        for head in range(GROUP):
            s = jnp.where(same, scores[:, head * rows : (head + 1) * rows], -1e30)
            e = jnp.exp(s - jnp.max(s, axis=1, keepdims=True))
            mixing.append((e / jnp.sum(e, axis=1, keepdims=True)).astype(BF16))
        o = dot(jnp.concatenate(mixing, axis=1), values)
        o = o.astype(BF16).reshape(frames // len(o_refs), len(o_refs), STEP, WIDE)
        for place, o_ref in enumerate(o_refs):
            o_ref[:, part, :] = o[:, place]


def temporal_fwd(x, weight, bias, local):
    frames, slots, width = x.shape
    groups = width // WIDE
    w = lambda part: pl.BlockSpec((width, WIDE), lambda g: (0, part * groups + g))
    b = lambda part: pl.BlockSpec((1, WIDE), lambda g: (0, part * groups + g))
    one = pl.BlockSpec((frames, slots, WIDE), lambda g: (0, 0, g))
    return pl.pallas_call(
        temporal_fwd_body,
        grid=(groups,),
        in_specs=[fixed(x.shape), w(0), w(1), w(2), b(0), b(1)],
        out_specs=[one] * 3 + [pl.BlockSpec((frames // local, slots, WIDE), lambda g: (0, 0, g))] * local,
        out_shape=[jax.ShapeDtypeStruct(x.shape, BF16)] * 3
        + [jax.ShapeDtypeStruct((frames // local, slots, width), BF16)] * local,
        cost_estimate=pl.CostEstimate(flops=30 * 10**9, bytes_accessed=16 * MIB, transcendentals=0),
        compiler_params=params(),
        name="temporal_fwd",
    )(x, weight, weight, weight, bias, bias)


def temporal_bwd_body(
    x_ref, q_ref, k_ref, v_ref, g_ref, wq_ref, wk_ref, wv_ref, gain_ref, shift_ref,
    dq_ref, dk_ref, dv_ref, dx_ref, sums_ref, norm_ref, total_ref,
):
    frames, slots, width = x_ref.shape
    rows = frames * STEP
    row = lax.broadcasted_iota(jnp.int32, (rows, rows), 0)
    col = lax.broadcasted_iota(jnp.int32, (rows, rows), 1)
    same = row % STEP == col % STEP
    shape = (frames, STEP, WIDE)
    for step in range(slots // STEP):
        part = slice(step * STEP, (step + 1) * STEP)
        k = k_ref[:, part, :].reshape(rows, WIDE)
        v = v_ref[:, part, :].reshape(rows, WIDE)
        queries = stacked(q_ref[:, part, :].reshape(rows, WIDE), rows)
        grads = stacked(g_ref[:, part, :].reshape(rows, WIDE), rows)
        scores = dot_nt(k, queries)
        grad_mixing = dot_nt(v, grads)
        mixing, grad_scores = [], []
        for head in range(GROUP):
            span = slice(head * rows, (head + 1) * rows)
            s = jnp.where(same, scores[:, span], -1e30)
            e = jnp.exp(s - jnp.max(s, axis=0, keepdims=True))
            p = e / jnp.sum(e, axis=0, keepdims=True)
            gp = grad_mixing[:, span]
            ds = p * (gp - jnp.sum(p * gp, axis=0, keepdims=True))
            mixing.append(p.astype(BF16))
            grad_scores.append(ds.astype(BF16))
        grad_scores = jnp.concatenate(grad_scores, axis=1)
        dv_ref[:, part, :] = dot(jnp.concatenate(mixing, axis=1), grads).astype(BF16).reshape(shape)
        dk_ref[:, part, :] = dot(grad_scores, queries).astype(BF16).reshape(shape)
        spread = dot_tn(grad_scores, k)
        dq = jnp.zeros((rows, WIDE), F32)
        for head in range(GROUP):
            dq = dq + spread[head * rows : (head + 1) * rows] * head_lanes(rows, head, F32)
        dq_ref[:, part, :] = (dq * HEAD_DIM**-0.5).astype(BF16).reshape(shape)
    flat = (frames * slots, WIDE)
    dq, dk, dv = dq_ref[...].reshape(flat), dk_ref[...].reshape(flat), dv_ref[...].reshape(flat)
    sums_ref[...] = jnp.concatenate([column_sum(dq), column_sum(dv), jnp.zeros((6, WIDE), F32)], axis=0)
    update = dot_nt(dq, wq_ref[...]) + dot_nt(dk, wk_ref[...]) + dot_nt(dv, wv_ref[...])
    group = pl.program_id(0)

    @pl.when(group == 0)
    def _():
        total_ref[...] = update

    @pl.when(group > 0)
    def _():
        total_ref[...] += update

    @pl.when(group == pl.num_programs(0) - 1)
    def _():
        total = total_ref[...]
        dx_ref[...] = total.astype(BF16).reshape(frames, slots, width)
        x = x_ref[...].reshape(frames * slots, width).astype(F32)
        shift_grad = column_sum(total)
        gain_grad = (column_sum(total * x) - shift_ref[...][None] * shift_grad) / gain_ref[...][None]
        norm_ref[...] = jnp.concatenate([gain_grad, shift_grad, jnp.zeros((6, width), F32)], axis=0)


def temporal_bwd(x, q, k, v, grad, weight, gain, shift):
    frames, slots, width = x.shape
    groups = width // WIDE
    w = lambda part: pl.BlockSpec((width, WIDE), lambda g: (0, part * groups + g))
    one = pl.BlockSpec((frames, slots, WIDE), lambda g: (0, 0, g))
    return pl.pallas_call(
        temporal_bwd_body,
        grid=(groups,),
        in_specs=[fixed(x.shape), one, one, one, one, w(0), w(1), w(2), fixed((width,)), fixed((width,))],
        out_specs=[one, one, one, fixed(x.shape), pl.BlockSpec((8, WIDE), lambda g: (0, g)), fixed((8, width))],
        out_shape=[jax.ShapeDtypeStruct(x.shape, BF16)] * 4 + [jax.ShapeDtypeStruct((8, width), F32)] * 2,
        scratch_shapes=[pltpu.VMEM((frames * slots, width), F32)],
        cost_estimate=pl.CostEstimate(flops=35 * 10**9, bytes_accessed=30 * MIB, transcendentals=0),
        compiler_params=params(),
        name="temporal_bwd",
    )(x, q, k, v, grad, weight, weight, weight, gain, shift)


def middle_body(mixed_ref, video_ref, proj_ref, pb_ref, gain_ref, shift_ref, w_ref, bias_ref, first_ref, normed_ref, qkv_ref):
    slots, width = video_ref.shape
    first = video_ref[...].astype(F32) + (dot(joined_positions(mixed_ref, slots), proj_ref[...]) + pb_ref[...])
    first_ref[...] = first
    unit, _ = norm_parts(first)
    normed_ref[...] = (unit * gain_ref[...] + shift_ref[...]).astype(BF16)
    normed = normed_ref[...]
    q = dot(normed, w_ref[:, :width]) + bias_ref[:, :width]
    qkv_ref[:, :width] = (q * HEAD_DIM**-0.5).astype(BF16)
    qkv_ref[:, width : 2 * width] = dot(normed, w_ref[:, width : 2 * width]).astype(BF16)
    qkv_ref[:, 2 * width :] = (dot(normed, w_ref[:, 2 * width :]) + bias_ref[:, width:]).astype(BF16)


def middle(frame, mixed, video, proj, proj_bias, gain, shift, weight, bias):
    _, slots, width = video.shape
    return pl.pallas_call(
        middle_body,
        grid=(1,),
        in_specs=[
            fixed(mixed.shape), pl.BlockSpec((None, slots, width), lambda i: (frame, 0, 0)), fixed(proj.shape), fixed((width,)),
            fixed((width,)), fixed((width,)), fixed(weight.shape), fixed((1, 2 * width)),
        ],
        out_specs=[fixed((slots, width)), fixed((slots, width)), fixed((slots, 3 * width))],
        out_shape=[
            jax.ShapeDtypeStruct((slots, width), F32),
            jax.ShapeDtypeStruct((slots, width), BF16),
            jax.ShapeDtypeStruct((slots, 3 * width), BF16),
        ],
        cost_estimate=pl.CostEstimate(flops=11 * 10**9, bytes_accessed=14 * MIB, transcendentals=0),
        compiler_params=params(),
        name="middle",
    )(mixed, video, proj, proj_bias, gain, shift, weight, bias)


def gelu_both(value):
    half = 0.5 * (1.0 + lax.erf(value * 0.7071067811865476))
    density = jnp.exp(-0.5 * value * value) * 0.3989422804014327
    return value * half, half + value * density


def feed_body(
    cot_ref, proj_ref, pb_ref, gain_ref, shift_ref, fc1_ref, fb1_ref, fc2_ref, fb2_ref, *refs, sub, frames,
):
    firsts, mixeds, refs = refs[:frames], refs[frames : 2 * frames], refs[2 * frames :]
    out_ref, normed_ref, hidden_ref, gi_ref, gs_ref, gso_ref, gspace_ref, sums_ref, unitsum_ref, second, branch, gnorm = refs
    frame, chunk = pl.program_id(0), pl.program_id(1)
    slots, width = cot_ref.shape
    units = fc1_ref.shape[1]
    for place in range(frames):

        @pl.when(jnp.logical_and(chunk == 0, frame == place))
        def _(place=place):
            second[...] = firsts[place][...] + (dot(mixeds[place][...], proj_ref[...]) + pb_ref[...])

    @pl.when(chunk == 0)
    def _():
        value = second[...]
        unit, _ = norm_parts(value)
        normed_ref[...] = (unit * gain_ref[...] + shift_ref[...]).astype(BF16)
        branch[...] = jnp.zeros_like(branch)
        gnorm[...] = jnp.zeros_like(gnorm)

    @pl.when(jnp.logical_and(frame == 0, chunk == 0))
    def _():
        sums_ref[...] = jnp.zeros_like(sums_ref)
        unitsum_ref[...] = jnp.zeros_like(unitsum_ref)

    normed = normed_ref[...]
    cot = cot_ref[...]
    for start in range(0, units, sub):
        span = slice(start, start + sub)
        inner = dot(normed, fc1_ref[:, span]) + fb1_ref[0:1, span]
        grad_hidden = dot(cot, fc2_ref[:, span])
        act, slope = gelu_both(inner)
        hidden_ref[:, span] = act.astype(BF16)
        gi_ref[:, span] = (grad_hidden * slope).astype(BF16)
    branch[...] += dot_nt(hidden_ref[...], fc2_ref[...])
    gnorm[...] += dot_nt(gi_ref[...], fc1_ref[...])
    unitsum_ref[chunk, 0:1, :] += column_sum(gi_ref[...])

    @pl.when(chunk == pl.num_programs(1) - 1)
    def _():
        value = second[...]
        out_ref[...] = (value + (branch[...] + fb2_ref[...])).astype(BF16)
        unit, scale = norm_parts(value)
        grad = gnorm[...]
        cot_full = cot_ref[...].astype(F32)
        grad_second = cot_full + norm_grad(grad, unit, scale, gain_ref[...])
        gs_ref[...] = grad_second
        gso_ref[...] = grad_second.astype(BF16)
        gspace_ref[...] = dot_nt(gso_ref[...], proj_ref[...]).astype(BF16)
        sums_ref[0:1, :] += column_sum(grad * unit)
        sums_ref[1:2, :] += column_sum(grad)
        sums_ref[2:3, :] += column_sum(gso_ref[...])
        sums_ref[3:4, :] += column_sum(cot_full)


def feed(first, mixed, cot, proj, proj_bias, gain, shift, joint, fc1_bias, fc2_bias, sub=None):
    frames, slots, width = cot.shape
    chunks, _, units = fc1_bias.shape
    sub = sub or units
    per = pl.BlockSpec((None, slots, width), lambda f, c: (f, 0, 0))
    row = fixed((width,))
    hid = pl.BlockSpec((None, None, slots, units), lambda f, c: (c, f, 0, 0))
    hid_shape = jax.ShapeDtypeStruct((chunks, frames, slots, units), BF16)
    tok = lambda dtype: jax.ShapeDtypeStruct(cot.shape, dtype)
    return pl.pallas_call(
        functools.partial(feed_body, sub=sub, frames=frames),
        grid=(frames, chunks),
        in_specs=[
            per, fixed(proj.shape), row, row, row,
            pl.BlockSpec((None, width, units), lambda f, c: (c, 0, 0)),
            pl.BlockSpec((None, 1, units), lambda f, c: (c, 0, 0)),
            pl.BlockSpec((None, width, units), lambda f, c: (c, 0, 1)),
            row,
        ] + [fixed((slots, width))] * (2 * frames),
        out_specs=[per, per, hid, hid, per, per, per, fixed((8, width)), fixed((chunks, 8, units))],
        out_shape=[
            tok(BF16), tok(BF16), hid_shape, hid_shape, tok(F32), tok(BF16), tok(BF16),
            jax.ShapeDtypeStruct((8, width), F32), jax.ShapeDtypeStruct((chunks, 8, units), F32),
        ],
        scratch_shapes=[pltpu.VMEM((slots, width), F32)] * 3,
        cost_estimate=pl.CostEstimate(flops=56 * 10**9, bytes_accessed=60 * MIB, transcendentals=0),
        compiler_params=params(60),
        name="feed",
    )(cot, proj, proj_bias, gain, shift, joint, fc1_bias, joint, fc2_bias, *first, *mixed)


def middle_bwd_body(
    dq_ref, dk_ref, dv_ref, w_ref, first_ref, gs_ref, gain_ref, proj_ref, gf_ref, gto_ref, gt_ref, sums_ref
):
    slots, width = first_ref.shape
    dq, dk, dv = dq_ref[...], dk_ref[...], dv_ref[...]
    grad = dot_nt(dq, w_ref[:, :width]) + dot_nt(dk, w_ref[:, width : 2 * width]) + dot_nt(dv, w_ref[:, 2 * width :])
    unit, scale = norm_parts(first_ref[...])
    grad_first = gs_ref[...] + norm_grad(grad, unit, scale, gain_ref[...])
    gf_ref[...] = grad_first
    gto_ref[...] = grad_first.astype(BF16)
    split_positions(gt_ref, dot_nt(gto_ref[...], proj_ref[...]).astype(BF16))

    rows = [grad * unit, grad, dq, dv, gto_ref[...]]
    sums_ref[...] = jnp.concatenate([column_sum(value) for value in rows] + [jnp.zeros((3, width), F32)], axis=0)


def middle_bwd(frame, dq, dk, dv, weight, first, grad_second, gain, proj, parts, share):
    slots, width = first.shape
    return pl.pallas_call(
        middle_bwd_body,
        grid=(1,),
        in_specs=[
            fixed((slots, width)), fixed((slots, width)), fixed((slots, width)), fixed(weight.shape), fixed((slots, width)),
            pl.BlockSpec((None, slots, width), lambda i: (frame, 0, 0)), fixed((width,)), fixed(proj.shape),
        ],
        out_specs=[fixed((slots, width)), fixed((slots, width)), fixed((parts, share, width)), fixed((8, width))],
        out_shape=[
            jax.ShapeDtypeStruct(first.shape, F32), jax.ShapeDtypeStruct(first.shape, BF16),
            jax.ShapeDtypeStruct((parts, share, width), BF16), jax.ShapeDtypeStruct((8, width), F32),
        ],
        cost_estimate=pl.CostEstimate(flops=14 * 10**9, bytes_accessed=16 * MIB, transcendentals=0),
        compiler_params=params(60),
        name="middle_bwd",
    )(dq, dk, dv, weight, first, grad_second, gain, proj)


def norm_out_body(grad_ref, video_ref, gain_ref, *refs):
    *gf_refs, out_ref = refs
    slots = video_ref.shape[0]
    frame = pl.program_id(0)
    unit, scale = norm_parts(video_ref[...].astype(F32))
    result = norm_grad(joined_positions(grad_ref, slots).astype(F32), unit, scale, gain_ref[...])
    for place, gf_ref in enumerate(gf_refs):

        @pl.when(frame == place)
        def _(gf_ref=gf_ref):
            out_ref[...] = gf_ref[...] + result


def norm_out(grad, video, grad_first, gain):
    frames, slots, width = video.shape
    per = lambda rows: pl.BlockSpec((None, rows, width), lambda f: (f, 0, 0))
    return pl.pallas_call(
        norm_out_body,
        grid=(frames,),
        in_specs=[by_part(grad.shape[0], grad.shape[2], width), per(slots), fixed((width,))]
        + [fixed((slots, width))] * frames,
        out_specs=per(slots),
        out_shape=jax.ShapeDtypeStruct(video.shape, F32),
        cost_estimate=pl.CostEstimate(flops=1 * 10**9, bytes_accessed=25 * MIB, transcendentals=0),
        compiler_params=params(),
        name="norm_out",
    )(grad, video, gain, *grad_first)


def tn_body(*refs):
    *refs, out_ref = refs
    count = len(refs) // 2
    total = None
    for a_ref, b_ref in zip(refs[:count], refs[count:]):
        rows, width = b_ref.shape[0], a_ref.shape[-1]
        part = dot_tn(a_ref[...].reshape(-1, width)[:rows], b_ref[...])
        total = part if total is None else total + part
    out_ref[...] = total.astype(out_ref.dtype)


def weight_grad(a, b):
    if isinstance(b, list):
        rows, width = b[0].shape
        places = [0] * len(b)
    else:
        rows, width = b.shape[0] // len(a), b.shape[1]
        places, b = range(len(a)), [b] * len(a)
    return pl.pallas_call(
        tn_body,
        grid=(width // WIDE,),
        in_specs=[fixed(value.shape) for value in a] + [pl.BlockSpec((rows, WIDE), lambda i, p=p: (p, i)) for p in places],
        out_specs=pl.BlockSpec((width, WIDE), lambda i: (0, i)),
        out_shape=jax.ShapeDtypeStruct((width, width), BF16),
        cost_estimate=pl.CostEstimate(
            flops=2 * len(b) * rows * width * width, bytes_accessed=4 * len(b) * rows * width, transcendentals=0
        ),
        compiler_params=params(),
        name="weight_grad",
    )(*a, *b)


def fc_grads_body(normed_ref, cot_ref, gi_ref, hid_ref, out_ref):
    units = gi_ref.shape[1]
    out_ref[:, :units] = dot_tn(normed_ref[...], gi_ref[...]).astype(BF16)
    out_ref[:, units:] = dot_tn(cot_ref[...], hid_ref[...]).astype(BF16)


def fc_grads(normed, cot, grad_inner, hidden):
    chunks, frames, slots, units = hidden.shape
    width = normed.shape[-1]
    rows = frames * slots
    hid = pl.BlockSpec((None, rows, units), lambda c: (c, 0, 0))
    flat = lambda value: value.reshape(chunks, rows, units)
    return pl.pallas_call(
        fc_grads_body,
        grid=(chunks,),
        in_specs=[fixed((rows, width)), fixed((rows, width)), hid, hid],
        out_specs=pl.BlockSpec((None, width, 2 * units), lambda c: (c, 0, 0)),
        out_shape=jax.ShapeDtypeStruct((chunks, width, 2 * units), BF16),
        cost_estimate=pl.CostEstimate(
            flops=4 * rows * width * units * chunks, bytes_accessed=4 * rows * units * chunks, transcendentals=0
        ),
        compiler_params=params(),
        name="fc_grads",
    )(normed.reshape(rows, width), cot.reshape(rows, width), flat(grad_inner), flat(hidden))


def finish_body(time_ref, space_ref, space_proj_ref, time_proj_ref, time_out, space_out, space_proj_out, time_proj_out):
    for group in range(time_ref.shape[0]):
        time_out[:, group * WIDE : (group + 1) * WIDE] = time_ref[group].astype(F32)
    space_out[...] = space_ref[...].astype(F32)

    @pl.when(pl.program_id(0) == 0)
    def _():
        space_proj_out[...] = space_proj_ref[...].astype(F32)
        time_proj_out[...] = time_proj_ref[...].astype(F32)


def finish(matrices):
    width = matrices.shape[1]
    groups = width // WIDE
    one = lambda at: pl.BlockSpec((None, width, width), lambda i: (at, 0, 0))
    block = pl.BlockSpec((width, width), lambda i: (0, i))
    full = jax.ShapeDtypeStruct((width, 3 * width), F32)
    square = jax.ShapeDtypeStruct((width, width), F32)
    return pl.pallas_call(
        finish_body,
        grid=(3,),
        in_specs=[
            pl.BlockSpec((groups, width, WIDE), lambda i: (0, 0, i)),
            pl.BlockSpec((None, width, width), lambda i: (groups + i, 0, 0)), one(groups + 3), one(groups + 4),
        ],
        out_specs=[block, block, fixed((width, width)), fixed((width, width))],
        out_shape=[full, full, square, square],
        cost_estimate=pl.CostEstimate(flops=1 * 10**9, bytes_accessed=30 * MIB, transcendentals=0),
        compiler_params=params(),
        name="finish",
    )(matrices, matrices, matrices, matrices)


MESH = pl.DeviceIdType.MESH
EARLY_GAP = 3.0
HOP = 4.0


def bits_of(count):
    return [1 << i for i in range(count.bit_length() - 1)]


def reducible(width, planes, parts):
    return parts == 4 and planes >= 4 and planes & (planes - 1) == 0 and width % (planes * 2 * 16) == 0


class Ring:
    def __init__(self, planes):
        self.bits = bits_of(planes)
        self.deep = len(self.bits)
        self.plane, self.part = lax.axis_index("dp"), lax.axis_index("mp")
        self.by_bit = {bit: {"dp": self.plane + bit - 2 * bit * self.place(bit)} for bit in self.bits}
        self.beside = {"mp": self.part + 1 - 2 * (self.part % 2)}
        self.across = {"mp": 3 - self.part}
        self.third = {"mp": (self.part + 2) % 4}
        self.inner = ((self.part + 1) // 2) % 2 == 1
        self.outer = ((self.part + 1) // 2) % 2 == 0
        self.started = []

    def place(self, bit):
        return (self.plane // bit) % 2

    def greet(self):
        partners = [self.by_bit[bit] for bit in self.bits] + [self.beside, self.across, self.third]
        barrier = pltpu.get_barrier_semaphore()
        for partner in partners:
            pl.semaphore_signal(barrier, inc=1, device_id=partner, device_id_type=MESH)
        pl.semaphore_wait(barrier, len(partners))

    def order(self, stream):
        return self.bits if stream == 0 else self.bits[:1] + self.bits[1:][::-1]

    def send(self, source, target, sems, at, partner, when=None):
        send_sem, recv_sem = sems
        copy = pltpu.make_async_remote_copy(
            src_ref=source, dst_ref=target, send_sem=send_sem.at[at], recv_sem=recv_sem.at[at],
            device_id=partner, device_id_type=MESH,
        )
        if when is None:
            copy.start()
        else:
            pl.when(when)(copy.start)
        self.started.append((when, copy))
        return copy

    def finish(self):
        for when, copy in self.started:
            if when is None:
                copy.wait_send()
            else:
                pl.when(when)(copy.wait_send)

    def rows(self, chain, level, width):
        stream = chain % 2
        mine = self.order(stream)
        size = width // 2
        spot, length = self.place(mine[0]) * size + stream * (size // 2), size // 2
        for bit in mine[1:level]:
            length //= 2
            spot = spot + self.place(bit) * length
        return spot, length


def rows_at(offset, size):
    return pl.ds(pl.multiple_of(offset, 16), size)


class Reduction:
    def __init__(self, ring, own, got, line, piece, out, spots, sems, back_sems, out_sem):
        self.ring, self.own, self.got, self.line, self.piece, self.sems = ring, own, got, line, piece, sems
        self.out, self.spots, self.back_sems, self.out_sem = out, spots, back_sems, out_sem
        self.width = own.shape[1]
        self.waiting = {}
        self.local = {}
        self.steps = 2 * ring.deep + 4

    def back(self, chain, step):
        ring, matrix = self.ring, chain // 2
        level = ring.deep - step
        if step == 0:
            spot, length = ring.rows(chain, level, self.width)
            source, region = self.piece.at[chain], self.out.at[self.spots[matrix], rows_at(spot, length)]
            self.local[chain] = pltpu.make_async_copy(source, region, self.out_sem.at[chain])
            self.local[chain].start()
        else:
            if step == 1:
                self.local[chain].wait()
            self.waiting[chain].wait_recv()
            if step == ring.deep:
                return
            spot, length = ring.rows(chain, level, self.width)
            source = region = self.out.at[self.spots[matrix], rows_at(spot, length)]
        partner = ring.by_bit[ring.order(chain % 2)[level - 1]]
        self.waiting[chain] = ring.send(source, region, self.back_sems, (chain, step), partner)

    def advance(self, chain, step):
        ring, deep = self.ring, self.ring.deep
        matrix, stream = chain // 2, chain % 2
        mine = ring.order(stream)
        size = self.width // 2
        got = self.got
        if step < deep or step == deep:
            if step == 0:
                spot = (1 - ring.place(mine[0])) * size + stream * (size // 2)
                source = self.own.at[matrix, rows_at(spot, size // 2)]
            else:
                self.waiting[chain].wait_recv()
                count = got[step - 1].shape[1]
                if step == 1:
                    kept = self.own[matrix, rows_at(ring.place(mine[0]) * size + stream * (size // 2), count), :]
                else:
                    kept = got[step - 2][chain, rows_at(ring.place(mine[step - 1]) * count, count), :]
                got[step - 1][chain] = (kept.astype(F32) + got[step - 1][chain].astype(F32)).astype(BF16)
                if step < deep:
                    half = count // 2
                    source = got[step - 1].at[chain, rows_at((1 - ring.place(mine[step])) * half, half)]
            if step < deep:
                self.waiting[chain] = ring.send(
                    source, got[step].at[chain], self.sems, (chain, step), ring.by_bit[mine[step]]
                )
                return
        if step <= deep + 3:
            self.line.advance(chain, step - deep, got[deep - 1].at[chain])
        if step >= deep + 3:
            self.back(chain, step - deep - 3)


class Line:
    def __init__(self, ring, lines, piece, sems, first=0):
        self.ring, self.lines, self.piece, self.sems, self.first = ring, lines, piece, sems, first
        self.waiting = {}

    def advance(self, chain, step, source):
        ring, lines, at = self.ring, self.lines, chain - self.first
        if step == 0:
            self.waiting[chain] = ring.send(source, lines[0].at[at], self.sems, (at, 0), ring.beside, ring.outer)
        elif step == 1:
            first = self.waiting[chain]

            @pl.when(ring.inner)
            def _():
                first.wait_recv()
                lines[0][at] = (source[...].astype(F32) + lines[0][at].astype(F32)).astype(BF16)

            self.waiting[chain] = ring.send(lines[0].at[at], lines[1].at[at], self.sems, (at, 1), ring.across, ring.inner)
        elif step == 2:
            second = self.waiting[chain]

            @pl.when(ring.inner)
            def _():
                second.wait_recv()
                both = (lines[0][at].astype(F32) + lines[1][at].astype(F32)).astype(BF16)
                self.piece[chain - self.first] = both
                lines[2][at] = both

            self.waiting[chain] = ring.send(lines[2].at[at], lines[3].at[at], self.sems, (at, 2), ring.beside, ring.inner)
        else:
            third = self.waiting[chain]

            @pl.when(ring.outer)
            def _():
                third.wait_recv()
                self.piece[chain - self.first] = lines[3][at]


def reduction_scratch(chains, width, deep):
    length = width // 4
    sizes = [length >> i for i in range(deep)]
    shapes = [pltpu.VMEM((chains, size, width), BF16) for size in sizes + [sizes[-1]] * 4]
    return shapes + [pltpu.SemaphoreType.DMA((chains, deep))] * 2 + [pltpu.SemaphoreType.DMA((chains, 3))] * 2 + [
        pltpu.SemaphoreType.DMA((chains, deep))
    ] * 2 + [pltpu.SemaphoreType.DMA((chains,)), pltpu.VMEM((chains, sizes[-1], width), BF16)]


def temporal_tail_body(
    gain_ref, shift_ref, small_in, *refs, planes, early, taken, local,
):
    g_refs, (x_hbm, q_hbm, k_hbm, v_hbm, w_hbm), refs = refs[:local], refs[local : local + 5], refs[local + 5 :]
    early_hbm, refs = refs[:early], refs[early:]
    moved_ref, out_ref, small_out, refs = refs[0], refs[1], refs[2], refs[3:]
    x_ref, qkv_ref, w_ref, d_ref, dx_ref, own, load_sem, refs = *refs[:7], refs[7:]
    move_send, move_recv, move_local, small_ref, small_got, small_held, small_send, small_recv, refs = *refs[:8], refs[8:]
    ring = Ring(planes)
    deep = ring.deep
    got, lines, refs = refs[:deep], refs[deep : deep + 4], refs[deep + 4 :]
    sems, line_sems, back_sems, out_sem, piece_ref = refs[:2], refs[2:4], refs[4:6], refs[6], refs[7]
    frames, slots, width = x_ref.shape
    groups = width // WIDE
    rows = frames * STEP
    loads = {}

    def load(name, source, target, at):
        copy = pltpu.make_async_copy(source, target, load_sem.at[at])
        copy.start()
        loads[name] = copy

    def load_group(group):
        for place, ref in enumerate((q_hbm, k_hbm, v_hbm)):
            source = ref.at[:, :, pl.ds(group * WIDE, WIDE)]
            load(("qkv", group, place), source, qkv_ref.at[group % 2, place], early + 2 + 3 * group + place)

    load_group(0)
    for matrix in range(early):
        load(("own", matrix), early_hbm[matrix], own.at[matrix], matrix)
    load("x", x_hbm, x_ref, early)
    load("w", w_hbm, w_ref, early + 1)
    ring.greet()
    matrices = early + groups
    line = Line(ring, lines, piece_ref, line_sems)
    spots = [groups + matrix for matrix in range(early)] + list(range(groups))
    sums = Reduction(ring, own, got, line, piece_ref, out_ref, spots, sems, back_sems, out_sem)
    small_ref[...] = small_in[...]

    row = lax.broadcasted_iota(jnp.int32, (rows, rows), 0)
    col = lax.broadcasted_iota(jnp.int32, (rows, rows), 1)
    same = row % STEP == col % STEP
    shape = (frames, STEP, WIDE)
    starts = {}
    ready = {}

    def compute():
        for group in range(groups):
            if group + 1 < groups:
                load_group(group + 1)
            for place in range(3):
                loads[("qkv", group, place)].wait()
            slot = group % 2
            lanes = slice(group * WIDE, (group + 1) * WIDE)
            for step in range(slots // STEP):
                part = slice(step * STEP, (step + 1) * STEP)
                k = qkv_ref[slot, 1, :, part, :].reshape(rows, WIDE)
                v = qkv_ref[slot, 2, :, part, :].reshape(rows, WIDE)
                queries = stacked(qkv_ref[slot, 0, :, part, :].reshape(rows, WIDE), rows)
                grads = jnp.stack([g_ref[:, part, lanes] for g_ref in g_refs], axis=1)
                grads = stacked(grads.reshape(rows, WIDE), rows)
                scores = dot_nt(k, queries)
                grad_mixing = dot_nt(v, grads)
                mixing, grad_scores = [], []
                for head in range(GROUP):
                    span = slice(head * rows, (head + 1) * rows)
                    s = jnp.where(same, scores[:, span], -1e30)
                    e = jnp.exp(s - jnp.max(s, axis=0, keepdims=True))
                    p = e / jnp.sum(e, axis=0, keepdims=True)
                    gp = grad_mixing[:, span]
                    ds = p * (gp - jnp.sum(p * gp, axis=0, keepdims=True))
                    mixing.append(p.astype(BF16))
                    grad_scores.append(ds.astype(BF16))
                grad_scores = jnp.concatenate(grad_scores, axis=1)
                dv = dot(jnp.concatenate(mixing, axis=1), grads)
                dk = dot(grad_scores, queries)
                spread = dot_tn(grad_scores, k)
                dq = jnp.zeros((rows, WIDE), F32)
                for head in range(GROUP):
                    dq = dq + spread[head * rows : (head + 1) * rows] * head_lanes(rows, head, F32)
                d_ref[group, :, part, :WIDE] = (dq * HEAD_DIM**-0.5).astype(BF16).reshape(shape)
                d_ref[group, :, part, WIDE : 2 * WIDE] = dk.astype(BF16).reshape(shape)
                d_ref[group, :, part, 2 * WIDE :] = dv.astype(BF16).reshape(shape)
                if step % 4 == 3:
                    yield 2.0
            if group == 0:
                loads["x"].wait()
            d = d_ref[group].reshape(frames * slots, 3 * WIDE)
            x = x_ref[...].reshape(frames * slots, width)
            own[early + group] = dot_tn(x, d).astype(BF16)
            ready[early + group] = True
            yield 4.5
            small_ref[taken : taken + 1, lanes] = column_sum(d[:, :WIDE])
            small_ref[taken + 1 : taken + 2, lanes] = column_sum(d[:, 2 * WIDE :])
        loads["w"].wait()
        quarter = frames // 4
        shift_grad, product = jnp.zeros((1, width), F32), jnp.zeros((1, width), F32)
        for distance in (2, 3, 1, 0):
            part = (ring.part + distance) % 4
            some = pl.ds(part * quarter, quarter)
            total = jnp.zeros((quarter * slots, width), F32)
            for group in range(groups):
                d = d_ref[group, some].reshape(quarter * slots, 3 * WIDE)
                for place in range(3):
                    weight = w_ref[:, pl.ds(place * width + group * WIDE, WIDE)]
                    total = total + dot_nt(d[:, place * WIDE : (place + 1) * WIDE], weight)
            dx_ref[some] = total.astype(BF16).reshape(quarter, slots, width)
            if distance:
                moves.append(move(distance))
                moves[-1].start()
            else:
                keep = pltpu.make_async_copy(dx_ref.at[some], moved_ref.at[ring.part], move_local.at[0])
                keep.start()
                kept.append(keep)
            x = x_ref[some].reshape(quarter * slots, width)
            shift_grad += column_sum(total)
            product += column_sum(total * x.astype(F32))
            yield 3.5
        small_ref[taken + 2 : taken + 3, :] = (product - shift_ref[...][None] * shift_grad) / gain_ref[...][None]
        small_ref[taken + 3 : taken + 4, :] = shift_grad

    moves, kept = [], []

    def move(distance, arriving=False):
        target = (ring.part + distance) % 4
        source = (ring.part + 4 - distance) % 4 if arriving else ring.part
        return pltpu.make_async_remote_copy(
            src_ref=dx_ref.at[pl.ds(target * (frames // 4), frames // 4)], dst_ref=moved_ref.at[source],
            send_sem=move_send.at[distance], recv_sem=move_recv.at[source], device_id={"mp": target}, device_id_type=MESH,
        )

    partners = [ring.by_bit[bit] for bit in ring.bits] + [ring.beside, ring.third]
    small_wait = []

    def small_step(step):
        if step > 0:
            small_wait.pop().wait_recv()
            before = small_ref[...] if step == 1 else small_held[step - 2]
            value = before + small_got[step - 1]
            if step == len(partners):
                small_out[...] = value
                return
            small_held[step - 1] = value
        source = small_ref if step == 0 else small_held.at[step - 1]
        small_wait.append(ring.send(source, small_got.at[step], (small_send, small_recv), step, partners[step]))

    following = [0] * matrices
    due = [EARLY_GAP * matrix for matrix in range(matrices)]
    clock = 0.0

    def advance_all():
        for matrix in range(matrices):
            step = following[matrix]
            if step < sums.steps and clock >= due[matrix] and (matrix < early or matrix in ready):
                if step == 0 and matrix < early:
                    loads[("own", matrix)].wait()
                for chain in (2 * matrix, 2 * matrix + 1):
                    sums.advance(chain, step)
                following[matrix] += 1
                due[matrix] = clock + HOP

    advance_all()
    for spent in compute():
        clock += spent
        advance_all()
    small_at = 0
    while any(step < sums.steps for step in following) or small_at <= len(partners):
        clock += HOP
        advance_all()
        if small_at <= len(partners):
            small_step(small_at)
            small_at += 1
    for distance in (1, 2, 3):
        move(distance, True).wait_recv()
    for copy in moves:
        copy.wait_send()
    kept[0].wait()
    ring.finish()


def temporal_tail(x, q, k, v, grad, weight, gain, shift, early, small, taken, planes, number):
    frames, slots, width = x.shape
    groups = width // WIDE
    deep = len(bits_of(planes))
    chains = 2 * (len(early) + groups)
    anywhere = pl.BlockSpec(memory_space=pl.ANY)
    whole = pl.BlockSpec(memory_space=pltpu.VMEM)
    flops = 2 * frames * slots * width * width * 12
    return pl.pallas_call(
        functools.partial(temporal_tail_body, planes=planes, early=len(early), taken=taken, local=len(grad)),
        in_specs=[whole] * (3 + len(grad)) + [anywhere] * (5 + len(early)),
        out_specs=[anywhere, anywhere, whole],
        out_shape=[
            jax.ShapeDtypeStruct((4, frames // 4, slots, width), BF16),
            jax.ShapeDtypeStruct((len(early) + groups, width, width), BF16),
            jax.ShapeDtypeStruct(small.shape, F32),
        ],
        scratch_shapes=[
            pltpu.VMEM(x.shape, BF16), pltpu.VMEM((2, 3, frames, slots, WIDE), BF16), pltpu.VMEM(weight.shape, BF16),
            pltpu.VMEM((groups, frames, slots, 3 * WIDE), BF16), pltpu.VMEM(x.shape, BF16),
            pltpu.VMEM((len(early) + groups, width, width), BF16),
            pltpu.SemaphoreType.DMA((len(early) + 2 + 3 * groups,)),
            pltpu.SemaphoreType.DMA((4,)), pltpu.SemaphoreType.DMA((4,)), pltpu.SemaphoreType.DMA((1,)),
            pltpu.VMEM(small.shape, F32), pltpu.VMEM((deep + 2,) + small.shape, F32), pltpu.VMEM((deep + 1,) + small.shape, F32),
            pltpu.SemaphoreType.DMA((deep + 2,)), pltpu.SemaphoreType.DMA((deep + 2,)),
        ] + reduction_scratch(chains, width, deep),
        cost_estimate=pl.CostEstimate(flops=flops, bytes_accessed=60 * MIB, transcendentals=0),
        compiler_params=pltpu.CompilerParams(vmem_limit_bytes=62 * MIB, collective_id=number, has_side_effects=True),
        name="temporal_tail",
    )(gain, shift, small, *grad, x, q, k, v, weight, *early)


def middle_and_space(frame, mixed, video, proj, proj_bias, gain, shift, weight, bias, patch_width):
    first, normed, qkv = middle(frame, mixed, video, proj, proj_bias, gain, shift, weight, bias)
    space_mixed, lse = spatial_fwd(patch_width, qkv, 1, video.shape[1])
    return first, normed, qkv, space_mixed, lse


def shards(
    video,
    patch_width,
    temporal_gain,
    temporal_shift,
    temporal_qkv,
    temporal_qv_bias,
    temporal_proj,
    temporal_proj_bias,
    spatial_gain,
    spatial_shift,
    spatial_qkv,
    spatial_qv_bias,
    spatial_proj,
    spatial_proj_bias,
    mlp_gain,
    mlp_shift,
    fc1_weight,
    fc1_bias,
    fc2_weight,
    fc2_bias,
    cotangent,
):
    frames, sets, slots, width = video.shape
    units = fc1_weight.shape[1]
    parts, planes = lax.axis_size("mp"), lax.axis_size("dp")
    share = -(-slots // (parts * STEP)) * STEP
    row = lambda value: value.astype(F32).reshape(1, -1)
    video = video.reshape(frames * sets, slots, width)
    cot = cotangent.reshape(frames * sets, slots, width)

    joint = jnp.concatenate([fc1_weight, fc2_weight.T], axis=1)
    piece = width // planes
    own = lax.dynamic_slice_in_dim(joint, lax.axis_index("dp") * piece, piece, 0)
    bias_rows = jnp.pad(fc1_bias.reshape(1, units), ((0, 15), (0, units)))
    own = jnp.concatenate([own, bias_rows], axis=0)[None]

    def exchange(value):
        return lax.all_to_all(value, "mp", split_axis=0, concat_axis=0, tiled=True)

    by_position = lambda value: value.reshape(parts * frames, share, width)
    by_device = lambda value: value.reshape(parts, frames, share, width)
    normed_in = norm_in(video, temporal_gain, temporal_shift, parts, share)
    x = by_position(exchange(normed_in))
    own, x = lax.optimization_barrier((own, x))
    column = lax.all_gather(own, "mp", axis=0, tiled=True)
    tq, tk, tv, *time_mixed = temporal_fwd(x, temporal_qkv, row(temporal_qv_bias), frames)
    column, *time_mixed = lax.optimization_barrier((column, *time_mixed))
    fb1 = column[:, piece : piece + 1, :units].astype(F32)
    joint = lax.all_gather(column[:, :piece], "dp", axis=1, tiled=True)
    time_back = [exchange(value) for value in time_mixed]

    several = lambda results: [list(values) for values in zip(*results)]
    spatial = []
    for f in range(frames):
        if f > 0:
            time_back[f], lse_before = lax.optimization_barrier((time_back[f], spatial[-1][-1]))
            spatial[-1] = spatial[-1][:-1] + (lse_before,)
        spatial.append(
            middle_and_space(
                f, time_back[f], video, temporal_proj, temporal_proj_bias, spatial_gain, spatial_shift, spatial_qkv,
                row(spatial_qv_bias), patch_width,
            )
        )
    first, normed_mid, space_qkv, space_mixed, lse = several(spatial)

    output, normed_out, hidden, grad_inner, grad_second, grad_space_out, grad_space, feed_sums, unit_sums = feed(
        first, [value[0] for value in space_mixed], cot, spatial_proj, spatial_proj_bias, mlp_gain, mlp_shift, joint, fb1, fc2_bias
    )
    fc_part = fc_grads(normed_out, cot, grad_inner, hidden)
    fc_part = lax.psum_scatter(fc_part, "dp", scatter_dimension=1, tiled=True)

    dq, dk, dv, grad_first, grad_time_out, mid_sums, grad_slot = [], [], [], [], [], [], []
    for f in range(frames):
        q_f, k_f, v_f = spatial_bwd(f, patch_width, space_qkv[f], space_mixed[f], lse[f], grad_space, 1, slots)
        if f > 0:
            grad_slot[-1], q_f = lax.optimization_barrier((grad_slot[-1], q_f))
        first_f, out_f, time_f, sums_f = middle_bwd(
            f, q_f[0], k_f[0], v_f[0], spatial_qkv, first[f], grad_second, spatial_gain, temporal_proj, parts, share
        )
        if f + 1 < frames:
            time_f, grad_space = lax.optimization_barrier((time_f, grad_space))
        grad_slot.append(exchange(time_f))
        for kept, value in zip(
            (dq, dk, dv, grad_first, grad_time_out, mid_sums), (q_f[0], k_f[0], v_f[0], first_f, out_f, sums_f)
        ):
            kept.append(value)
    early = [
        weight_grad(normed_mid, dq),
        weight_grad(normed_mid, dk),
        weight_grad(normed_mid, dv),
        weight_grad([value[0] for value in space_mixed], grad_space_out.reshape(-1, width)),
        weight_grad(time_back, grad_time_out),
    ]
    fc_part, grad_first[-1] = lax.optimization_barrier((fc_part, grad_first[-1]))
    fc_part = lax.psum_scatter(fc_part, "mp", scatter_dimension=0, tiled=True)[0].astype(F32)
    fc1_weight_grad = fc_part[:, :units]
    fc2_weight_grad = fc_part[:, units:].T

    own_sums = [unit_sums[:, 0, :].reshape(-1, width), feed_sums[:4], sum(mid_sums)[:5]]
    weights = (temporal_qkv, temporal_gain, temporal_shift)
    wide = lambda blocks: jnp.concatenate([block.astype(F32) for block in blocks], axis=1)
    if reducible(width, planes, parts):
        taken = sum(rows.shape[0] for rows in own_sums)
        small = jnp.concatenate(own_sums + [jnp.zeros((4 + -(taken + 4) % 8, width), F32)], axis=0)
        grad_in, matrices, small = temporal_tail(x, tq, tk, tv, grad_slot, *weights, early, small, taken, planes, 1)
        temporal_qkv_grad, spatial_qkv_grad, spatial_proj_grad, temporal_proj_grad = finish(matrices)
    else:
        gq, gk, gv, grad_x, bias_sums, norm_sums = temporal_bwd(x, tq, tk, tv, by_position(jnp.stack(grad_slot, axis=1)), *weights)
        grad_in = exchange(by_device(grad_x))
        small = jnp.concatenate(own_sums + [bias_sums[:2], norm_sums[:2]], axis=0)
        flat = lambda value: value.reshape(-1, width)
        late = [weight_grad([flat(x)], [flat(value)]) for value in (gq, gk, gv)]
        matrices, small = lax.psum((jnp.stack(early + late), small), ("dp", "mp"))
        temporal_qkv_grad = wide([matrices[5 + p] for p in range(3)])
        spatial_qkv_grad = wide([matrices[p] for p in range(3)])
        spatial_proj_grad, temporal_proj_grad = matrices[3].astype(F32), matrices[4].astype(F32)
    video_grad = norm_out(grad_in, video, grad_first, temporal_gain)
    count = parts * units // width
    fc1_bias_grad = small[:count].reshape(-1)
    (
        mlp_gain_grad, mlp_shift_grad, spatial_proj_bias_grad, fc2_bias_grad,
        spatial_gain_grad, spatial_shift_grad, space_q_sum, space_v_sum, temporal_proj_bias_grad,
        time_q_sum, time_v_sum, temporal_gain_grad, temporal_shift_grad,
    ) = [small[count + i] for i in range(13)]
    return (
        output.reshape(frames, sets, slots, width),
        video_grad.reshape(frames, sets, slots, width),
        temporal_gain_grad,
        temporal_shift_grad,
        temporal_qkv_grad,
        jnp.concatenate([time_q_sum, time_v_sum]),
        temporal_proj_grad,
        temporal_proj_bias_grad,
        spatial_gain_grad,
        spatial_shift_grad,
        spatial_qkv_grad,
        jnp.concatenate([space_q_sum, space_v_sum]),
        spatial_proj_grad,
        spatial_proj_bias_grad,
        mlp_gain_grad,
        mlp_shift_grad,
        fc1_weight_grad,
        fc1_bias_grad,
        fc2_weight_grad,
        fc2_bias_grad,
    )


def solution(mesh):
    tokens = P("mp", "dp", None, None)
    return jax.shard_map(
        shards,
        mesh=mesh,
        in_specs=(tokens, P("dp")) + (P(),) * 14 + (P(None, "mp"), P("mp"), P("mp", None), P(), tokens),
        out_specs=(tokens, tokens) + (P(),) * 14 + (P("dp", "mp"), P(), P("mp", "dp"), P()),
        check_vma=False,
    )
```

profile of v0, /device:TPU:0, one launch (start us, length us, event | category | flops | bytes accessed | tf_op | source)
XLA Modules:
  0.0 582.5 jit_solution(7028898171251007885)
XLA Ops:
  7.2 4.1 norm_in.1
  11.3 6.4 %all-to-all-start = ((bf16[4,2,208,768]{3,2,1,0:T(8,128)(2,1)}), bf16[4,2,208,768]{3,2,1,0:T(8,128)(2,1)}, u32[]{:S(2)}, u32[]{:S(2)}) async-start(bf16[4,2,208,768]{3,2,1,0:T(8,128)(2,1)} %norm_in.1), calls=%async_computation | async-start | bytes 5111808 | tf_op jit(solution)/shard_map/all_to_all | solution.py:1112
  19.9 56.0 %all-to-all-done = bf16[4,2,208,768]{3,2,1,0:T(8,128)(2,1)} async-done(((bf16[4,2,208,768]{3,2,1,0:T(8,128)(2,1)}), bf16[4,2,208,768]{3,2,1,0:T(8,128)(2,1)}, u32[]{:S(2)}, u32[]{:S(2)}) %all-to-all-start) | async-done | bytes 2555936 | tf_op jit(solution)/shard_map/all_to_all | solution.py:1112
  75.9 28.4 %temporal_fwd.1 = (bf16[8,208,768]{2,1,0:T(8,128)(2,1)}, bf16[8,208,768]{2,1,0:T(8,128)(2,1)}, bf16[8,208,768]{2,1,0:T(8,128)(2,1)}, bf16[4,208,768]{2,1,0:T(8,128)(2,1)}, bf16[4,208,768]{2,1,0:T(8,128)(2,1)}) custom-call(bf16[8,208,768]{2,1,0:T(8,128)(2,1)} %bitcast.4.x_ref.refs_2_, bf16[768,2304]{1,0:T(8,128)(2,1)} %refs_6_.1, bf16[768,2304]{1,0:T(8,128)(2,1)} %refs_6_.1, ...), custom_call_target="tpu_custom_call" | custom-call | flops 30000001024 | bytes 16777216 | tf_op jit(solution)/shard_map/temporal_fwd/pallas_call | solution.py:300
  104.3 4.7 all-gather.3.cloned.1.call-done
  109.0 2.4 slice.63
  111.4 3.5 all-to-all-start.1
  116.2 1.4 slice_convert_fusion.fb1_ref
  117.6 27.5 %all-to-all-done.1.mixed_ref.refs_0_ = bf16[4,208,768]{2,1,0:T(8,128)(2,1)S(1)} async-done(((bf16[4,208,768]{2,1,0:T(8,128)(2,1)}), bf16[4,208,768]{2,1,0:T(8,128)(2,1)S(1)}, u32[]{:S(2)}, u32[]{:S(2)}) %all-to-all-start.1) | async-done | bytes 1277984 | tf_op jit(solution)/shard_map/all_to_all | solution.py:1112
  145.1 3.5 all-to-all-start.2
  148.7 10.1 %middle.2 = (f32[784,768]{1,0:T(8,128)}, bf16[784,768]{1,0:T(8,128)(2,1)}, bf16[784,2304]{1,0:T(8,128)(2,1)}) custom-call(bf16[4,208,768]{2,1,0:T(8,128)(2,1)} %copy-done, bf16[2,784,768]{2,1,0:T(8,128)(2,1)} %bitcast.35, bf16[768,768]{1,0:T(8,128)(2,1)} %proj_ref.9, f32[768]{0:T(1024)} %pb_ref.4, f32[768]{0:T(1024)} %gain_ref.13, f32[768]{0:T(1024)} %shift_ref.7, ...), custom_call_target="tpu_custom_call" | custom-call | flops 11000000512 | bytes 14680064 | tf_op jit(solution)/shard_map/middle/pallas_call | solution.py:406
  158.7 17.1 %spatial_fwd.2 = (bf16[1,784,768]{2,1,0:T(8,128)(2,1)}, f32[1,3,8,784]{3,2,1,0:T(8,128)}) custom-call(s32[1]{0:T(128)S(6)} %copy.49.width_ref, bf16[1,784,2304]{2,1,0:T(8,128)(2,1)} %bitcast.56, bf16[1,784,2304]{2,1,0:T(8,128)(2,1)} %bitcast.57, bf16[1,784,2304]{2,1,0:T(8,128)(2,1)} %bitcast.58), custom_call_target="tpu_custom_call" | custom-call | flops 20000000000 | bytes 5242880 | tf_op jit(solution)/shard_map/spatial_fwd/pallas_call | solution.py:95
  175.8 2.9 all-to-all-done.2.mixed_ref.refs_1_
  178.7 1.0 copy-done.1
  179.8 9.9 %middle.3 = (f32[784,768]{1,0:T(8,128)}, bf16[784,768]{1,0:T(8,128)(2,1)}, bf16[784,2304]{1,0:T(8,128)(2,1)}) custom-call(bf16[4,208,768]{2,1,0:T(8,128)(2,1)} %copy-done.1, bf16[2,784,768]{2,1,0:T(8,128)(2,1)} %bitcast.36, bf16[768,768]{1,0:T(8,128)(2,1)} %proj_ref.9, f32[768]{0:T(1024)} %pb_ref.4, f32[768]{0:T(1024)} %gain_ref.13, f32[768]{0:T(1024)} %shift_ref.7, ...), custom_call_target="tpu_custom_call" | custom-call | flops 11000000512 | bytes 14680064 | tf_op jit(solution)/shard_map/middle/pallas_call | solution.py:406
  189.7 17.4 %spatial_fwd.3 = (bf16[1,784,768]{2,1,0:T(8,128)(2,1)}, f32[1,3,8,784]{3,2,1,0:T(8,128)}) custom-call(s32[1]{0:T(128)S(6)} %copy.49.width_ref, bf16[1,784,2304]{2,1,0:T(8,128)(2,1)} %bitcast.50, bf16[1,784,2304]{2,1,0:T(8,128)(2,1)} %bitcast.51, bf16[1,784,2304]{2,1,0:T(8,128)(2,1)} %bitcast.52), custom_call_target="tpu_custom_call" | custom-call | flops 20000000000 | bytes 5242880 | tf_op jit(solution)/shard_map/spatial_fwd/pallas_call | solution.py:95
  207.1 51.5 %feed.1 = (bf16[2,784,768]{2,1,0:T(8,128)(2,1)}, bf16[2,784,768]{2,1,0:T(8,128)(2,1)}, bf16[4,2,784,768]{3,2,1,0:T(8,128)(2,1)}, bf16[4,2,784,768]{3,2,1,0:T(8,1...) custom-call(bf16[2,784,768]{2,1,0:T(8,128)(2,1)} %bitcast.46, ...), custom_call_target="tpu_custom_call" | custom-call | flops 56000000000 | bytes 62914560 | tf_op jit(solution)/shard_map/feed/pallas_call | solution.py:497
  258.6 23.1 %fc_grads.1 = bf16[4,768,1536]{2,1,0:T(8,128)(2,1)} custom-call(bf16[1568,768]{1,0:T(8,128)(2,1)} %bitcast.63, bf16[1568,768]{1,0:T(8,128)(2,1)} %bitcast.47, bf16[4,1568,768]{2,1,0:T(8,128)(2,1)} %bitcast.49, bf16[4,1568,768]{2,1,0:T(8,128)(2,1)} %bitcast.48), custom_call_target="tpu_custom_call" | custom-call | flops 14797504512 | bytes 19267584 | tf_op jit(solution)/shard_map/fc_grads/pallas_call | solution.py:628
  281.7 28.7 %spatial_bwd.2 = (bf16[1,784,768]{2,1,0:T(8,128)(2,1)}, bf16[1,784,768]{2,1,0:T(8,128)(2,1)}, bf16[1,784,768]{2,1,0:T(8,128)(2,1)}) custom-call(s32[1]{0:T(128)S(6)} %copy.49.width_ref, bf16[1,784,2304]{2,1,0:T(8,128)(2,1)} %bitcast.59, bf16[1,784,2304]{2,1,0:T(8,128)(2,1)} %bitcast.60, bf16[1,784,2304]{2,1,0:T(8,128)(2,1)} %bitcast.61, ...), custom_call_target="tpu_custom_call" | custom-call | flops 32000000000 | bytes 9437184 | tf_op jit(solution)/shard_map/spatial_bwd/pallas_call | solution.py:175
  310.5 12.8 %middle_bwd.2 = (f32[784,768]{1,0:T(8,128)}, bf16[784,768]{1,0:T(8,128)(2,1)}, bf16[4,208,768]{2,1,0:T(8,128)(2,1)}, f32[8,768]{1,0:T(8,128)}) custom-call(bf16[784,768]{1,0:T(8,128)(2,1)} %bitcast.64, bf16[784,768]{1,0:T(8,128)(2,1)} %bitcast.66, bf16[784,768]{1,0:T(8,128)(2,1)} %bitcast.68, bf16[768,2304]{1,0:T(8,128)(2,1)} %w_ref.7, ...), custom_call_target="tpu_custom_call" | custom-call | flops 14000000000 | bytes 16777216 | tf_op jit(solution)/shard_map/middle_bwd/pallas_call | solution.py:537
  323.3 3.6 all-to-all-start.3
  326.9 28.7 %spatial_bwd.3 = (bf16[1,784,768]{2,1,0:T(8,128)(2,1)}, bf16[1,784,768]{2,1,0:T(8,128)(2,1)}, bf16[1,784,768]{2,1,0:T(8,128)(2,1)}) custom-call(s32[1]{0:T(128)S(6)} %copy.49.width_ref, bf16[1,784,2304]{2,1,0:T(8,128)(2,1)} %bitcast.53, bf16[1,784,2304]{2,1,0:T(8,128)(2,1)} %bitcast.54, bf16[1,784,2304]{2,1,0:T(8,128)(2,1)} %bitcast.55, ...), custom_call_target="tpu_custom_call" | custom-call | flops 32000000000 | bytes 9437184 | tf_op jit(solution)/shard_map/spatial_bwd/pallas_call | solution.py:175
  355.5 13.0 %middle_bwd.3 = (f32[784,768]{1,0:T(8,128)}, bf16[784,768]{1,0:T(8,128)(2,1)}, bf16[4,208,768]{2,1,0:T(8,128)(2,1)}, f32[8,768]{1,0:T(8,128)}) custom-call(bf16[784,768]{1,0:T(8,128)(2,1)} %bitcast.70, bf16[784,768]{1,0:T(8,128)(2,1)} %bitcast.72, bf16[784,768]{1,0:T(8,128)(2,1)} %bitcast.74, bf16[768,2304]{1,0:T(8,128)(2,1)} %w_ref.7, ...), custom_call_target="tpu_custom_call" | custom-call | flops 14000000000 | bytes 16777216 | tf_op jit(solution)/shard_map/middle_bwd/pallas_call | solution.py:537
  368.6 5.2 all-to-all-start.4
  373.9 6.0 %weight_grad.7.refs_9_ = bf16[768,768]{1,0:T(8,128)(2,1)} custom-call(bf16[784,768]{1,0:T(8,128)(2,1)} %get-tuple-element.117.refs_0_, bf16[784,768]{1,0:T(8,128)(2,1)} %get-tuple-element.118.refs_1_, bf16[784,768]{1,0:T(8,128)(2,1)} %bitcast.69, bf16[784,768]{1,0:T(8,128)(2,1)} %bitcast.75), custom_call_target="tpu_custom_call" | custom-call | flops 1849688064 | bytes 4816896 | tf_op jit(solution)/shard_map/weight_grad/pallas_call | solution.py:602
  379.9 6.1 %weight_grad.6.refs_8_ = bf16[768,768]{1,0:T(8,128)(2,1)} custom-call(bf16[784,768]{1,0:T(8,128)(2,1)} %get-tuple-element.117.refs_0_, bf16[784,768]{1,0:T(8,128)(2,1)} %get-tuple-element.118.refs_1_, bf16[784,768]{1,0:T(8,128)(2,1)} %bitcast.67, bf16[784,768]{1,0:T(8,128)(2,1)} %bitcast.73), custom_call_target="tpu_custom_call" | custom-call | flops 1849688064 | bytes 4816896 | tf_op jit(solution)/shard_map/weight_grad/pallas_call | solution.py:602
  386.0 6.0 %weight_grad.8.refs_10_ = bf16[768,768]{1,0:T(8,128)(2,1)} custom-call(bf16[784,768]{1,0:T(8,128)(2,1)} %bitcast.43, bf16[784,768]{1,0:T(8,128)(2,1)} %bitcast.45, bf16[1568,768]{1,0:T(8,128)(2,1)} %bitcast.38, bf16[1568,768]{1,0:T(8,128)(2,1)} %bitcast.39), custom_call_target="tpu_custom_call" | custom-call | flops 1849688064 | bytes 4816896 | tf_op jit(solution)/shard_map/weight_grad/pallas_call | solution.py:602
  392.0 6.0 %weight_grad.5.refs_7_ = bf16[768,768]{1,0:T(8,128)(2,1)} custom-call(bf16[784,768]{1,0:T(8,128)(2,1)} %get-tuple-element.117.refs_0_, bf16[784,768]{1,0:T(8,128)(2,1)} %get-tuple-element.118.refs_1_, bf16[784,768]{1,0:T(8,128)(2,1)} %bitcast.65, bf16[784,768]{1,0:T(8,128)(2,1)} %bitcast.71), custom_call_target="tpu_custom_call" | custom-call | flops 1849688064 | bytes 4816896 | tf_op jit(solution)/shard_map/weight_grad/pallas_call | solution.py:602
  398.0 6.5 %weight_grad.9.refs_11_ = bf16[768,768]{1,0:T(8,128)(2,1)} custom-call(bf16[4,208,768]{2,1,0:T(8,128)(2,1)} %copy-done, bf16[4,208,768]{2,1,0:T(8,128)(2,1)} %copy-done.1, bf16[784,768]{1,0:T(8,128)(2,1)} %get-tuple-element.120.refs_2_, bf16[784,768]{1,0:T(8,128)(2,1)} %get-tuple-element.121.refs_3_), custom_call_target="tpu_custom_call" | custom-call | flops 1849688064 | bytes 4816896 | tf_op jit(solution)/shard_map/weight_grad/pallas_call | solution.py:602
  406.3 146.2 %temporal_tail.1 = (bf16[4,2,208,768]{3,2,1,0:T(8,128)(2,1)}, bf16[8,768,768]{2,1,0:T(8,128)(2,1)}, f32[24,768]{1,0:T(8,128)}) custom-call(f32[768]{0:T(1024)} %gain_ref.15, f32[768]{0:T(1024)} %shift_ref.9, f32[24,768]{1,0:T(8,128)} %maximum_maximum_fusion.small_in, bf16[4,208,768]{2,1,0:T(8,128)(2,1)} %copy-done.2, bf16[4,208,768]{2,1,0:T(8,128)(2,1)} %copy-done.3, ...), custom_call_target="tpu_custom_call" | custom-call | flops 23555211264 | bytes 62914560 | tf_op jit(solution)/shard_map/temporal_tail/pallas_call | solution.py:1044
  553.9 10.3 %finish.1 = (f32[768,2304]{1,0:T(8,128)}, f32[768,2304]{1,0:T(8,128)}, f32[768,768]{1,0:T(8,128)}, f32[768,768]{1,0:T(8,128)}) custom-call(bf16[8,768,768]{2,1,0:T(8,128)(2,1)} %get-tuple-element.130.time_ref.space_ref.space_proj_ref.time_proj_ref, bf16[8,768,768]{2,1,0:T(8,128)(2,1)} %get-tuple-element.130.time_ref.space_ref.space_proj_ref.time_proj_ref, ...), custom_call_target="tpu_custom_call" | custom-call | flops 1000000000 | bytes 31457280 | tf_op jit(solution)/shard_map/finish/pallas_call | solution.py:660
  565.5 8.1 %norm_out.1 = f32[2,784,768]{2,1,0:T(8,128)} custom-call(bf16[4,2,208,768]{3,2,1,0:T(8,128)(2,1)} %get-tuple-element.122.grad_ref, bf16[2,784,768]{2,1,0:T(8,128)(2,1)} %bitcast.37, f32[768]{0:T(1024)} %gain_ref.15, f32[784,768]{1,0:T(8,128)} %get-tuple-element.123.refs_0_, f32[784,768]{1,0:T(8,128)} %get-tuple-element.128.refs_1_), custom_call_target="tpu_custom_call" | custom-call | flops 1000000000 | bytes 26214400 | tf_op jit(solution)/shard_map/norm_out/pallas_call | solution.py:571
  (59 shorter events, 9.3 us)
Async XLA Ops:
  11.3 6.5 %copy-start.4 = (bf16[768,768]{1,0:T(8,128)(2,1)S(1)}, bf16[768,768]{1,0:T(8,128)(2,1)}, u32[]{:S(2)}) copy-start(bf16[768,768]{1,0:T(8,128)(2,1)} %param.39) | copy-start | bytes 3538948
  11.3 64.6 %all-to-all-start = ((bf16[4,2,208,768]{3,2,1,0:T(8,128)(2,1)}), bf16[4,2,208,768]{3,2,1,0:T(8,128)(2,1)}, u32[]{:S(2)}, u32[]{:S(2)}) async-start(bf16[4,2,208,768]{3,2,1,0:T(8,128)(2,1)} %norm_in.1), calls=%async_computation | async-start | bytes 5111808 | tf_op jit(solution)/shard_map/all_to_all | solution.py:1112
  17.7 0.7 copy-start.13
  17.7 0.8 copy-start.10
  17.7 1.4 copy-start.5
  17.7 91.2 %all-gather.3.cloned.1.call-start = ((), (), s32[]{:S(2)}) async-start(), calls=%async_computation.7 | async-start | bytes 1720320 | tf_op jit(solution)/shard_map/all_gather | solution.py:1119
  75.9 131.2 %all-gather.5.cloned.1.call-start = ((), (), s32[]{:S(2)}) async-start(), calls=%async_computation.8 | async-start | bytes 10616832 | tf_op jit(solution)/shard_map/all_gather | solution.py:1123
  111.3 3.6 copy-start.11
  111.4 33.7 %all-to-all-start.1 = ((bf16[4,208,768]{2,1,0:T(8,128)(2,1)}), bf16[4,208,768]{2,1,0:T(8,128)(2,1)S(1)}, u32[]{:S(2)}, u32[]{:S(2)}) async-start(bf16[4,208,768]{2,1,0:T(8,128)(2,1)} %get-tuple-element.83), calls=%async_computation.1 | async-start | bytes 2555904 | tf_op jit(solution)/shard_map/all_to_all | solution.py:1112
  145.1 3.6 copy-start
  145.1 33.6 %all-to-all-start.2 = ((bf16[4,208,768]{2,1,0:T(8,128)(2,1)}), bf16[4,208,768]{2,1,0:T(8,128)(2,1)S(1)}, u32[]{:S(2)}, u32[]{:S(2)}) async-start(bf16[4,208,768]{2,1,0:T(8,128)(2,1)} %get-tuple-element.85), calls=%async_computation.2 | async-start | bytes 2555904 | tf_op jit(solution)/shard_map/all_to_all | solution.py:1112
  148.6 256.6 %reduce-scatter.3.cloned.1.call-start = ((), (), s32[]{:S(2)}) async-start(), calls=%async_computation.9 | async-start | bytes 10616832 | tf_op jit(solution)/shard_map/reduce_scatter | solution.py:1144
  178.7 1.0 copy-start.1
  323.3 32.2 %all-to-all-start.3 = ((bf16[4,208,768]{2,1,0:T(8,128)(2,1)}), bf16[4,208,768]{2,1,0:T(8,128)(2,1)S(1)}, u32[]{:S(2)}, u32[]{:S(2)}) async-start(bf16[4,208,768]{2,1,0:T(8,128)(2,1)} %get-tuple-element.104), calls=%async_computation.3 | async-start | bytes 2555904 | tf_op jit(solution)/shard_map/all_to_all | solution.py:1112
  355.5 13.0 %copy-start.2 = (bf16[4,208,768]{2,1,0:T(8,128)(2,1)}, bf16[4,208,768]{2,1,0:T(8,128)(2,1)S(1)}, u32[]{:S(2)}) copy-start(bf16[4,208,768]{2,1,0:T(8,128)(2,1)S(1)} %all-to-all-done.3.refs_0_) | copy-start | bytes 3833860
  368.6 5.3 copy-start.6
  368.6 5.3 copy-start.12
  368.6 36.7 %all-to-all-start.4 = ((bf16[4,208,768]{2,1,0:T(8,128)(2,1)}), bf16[4,208,768]{2,1,0:T(8,128)(2,1)S(1)}, u32[]{:S(2)}, u32[]{:S(2)}) async-start(bf16[4,208,768]{2,1,0:T(8,128)(2,1)} %get-tuple-element.113), calls=%async_computation.4 | async-start | bytes 2555904 | tf_op jit(solution)/shard_map/all_to_all | solution.py:1112
  373.8 199.8 %reduce-scatter.5.cloned.1.call-start = ((), (), s32[]{:S(2)}) async-start(), calls=%async_computation.10 | async-start | bytes 1474560 | tf_op jit(solution)/shard_map/reduce_scatter | solution.py:1169
  398.0 6.5 %copy-start.8 = (f32[8,768]{1,0:T(8,128)S(1)}, f32[8,768]{1,0:T(8,128)}, u32[]{:S(2)}) copy-start(f32[8,768]{1,0:T(8,128)} %get-tuple-element.102) | copy-start | bytes 73732
  398.0 6.5 %copy-start.9 = (f32[8,768]{1,0:T(8,128)S(1)}, f32[8,768]{1,0:T(8,128)}, u32[]{:S(2)}) copy-start(f32[8,768]{1,0:T(8,128)} %get-tuple-element.111) | copy-start | bytes 73732
  405.3 1.0 copy-start.3
  553.9 10.4 %copy-start.7 = (f32[24,768]{1,0:T(8,128)S(1)}, f32[24,768]{1,0:T(8,128)}, u32[]{:S(2)}) copy-start(f32[24,768]{1,0:T(8,128)} %get-tuple-element.129) | copy-start | bytes 221188
Sparse Core Ops, SparseCore 0:
  76.0 32.8 all-gather.2
  111.5 57.8 all-gather.4
  281.9 74.6 reduce-scatter.2
  405.4 33.3 reduce-scatter.4
where the time goes:
time: 592 us; the launch traced here: 582 us
  Pallas kernels  440 us (74%)
  waiting for transfers between devices  91.1 us (15%)
  starting transfers between devices  22.4 us (4%)
  between operations  15.1 us (3%)
  local copies, waits for them, and re-layouts  9.37 us (2%)
    pallas_call x1, Pallas kernels, temporal_tail(): pl.pallas_call(functools.partial(temporal_tail_body, planes=planes, early...  146 us
    all_to_all x5, waiting for transfers between devices, exchange(): return lax.all_to_all(value, 'mp', split_axis=0, concat_axis=0, tiled=True)  86.4 us
    pallas_call x2, Pallas kernels, spatial_bwd(): pl.pallas_call(functools.partial(spatial_bwd_body, slots=slots, rows=rows...  57.4 us
    pallas_call x1, Pallas kernels, feed(): pl.pallas_call(functools.partial(feed_body, sub=sub, frames=frames), grid...  51.5 us
    pallas_call x2, Pallas kernels, spatial_fwd(): pl.pallas_call(functools.partial(spatial_fwd_body, slots=slots, rows=rows...  34.5 us
    pallas_call x5, Pallas kernels, weight_grad(): pl.pallas_call(tn_body, grid=(width // WIDE,), in_specs=[fixed(value.shap...  30.6 us
    pallas_call x1, Pallas kernels, temporal_fwd(): pl.pallas_call(temporal_fwd_body, grid=(groups,), in_specs=[fixed(x.shape...  28.4 us
    pallas_call x2, Pallas kernels, middle_bwd(): pl.pallas_call(middle_bwd_body, grid=(1,), in_specs=[fixed((slots, width)...  25.8 us
  transfers between devices with their start and end apart: 9, of which 4 were waited for; matrix products, arithmetic and copies ran while one was open for 1% of the time, Pallas kernels for 62%

commit v1 on v0

--- a/solution.py
+++ b/solution.py
@@ -1065,6 +1065,136 @@
     )(gain, shift, small, *grad, x, q, k, v, weight, *early)
 
 
+def temporal_head_body(video_ref, gain_ref, shift_ref, w_ref, bias_ref, *refs, chunks, local):
+    x_out, q_out, k_out, v_out, refs = *refs[:4], refs[4:]
+    o_outs, refs = refs[:local], refs[local:]
+    normed, xs, qs, ks, vs, os, send_sem, recv_sem, out_sem = refs
+    ring = Ring(lax.axis_size("dp"))
+    me = ring.part
+    frames, share, width = xs.shape
+    slots = video_ref.shape[1]
+    groups = width // WIDE
+    barrier = pltpu.get_barrier_semaphore()
+    for partner in (ring.beside, ring.across, ring.third):
+        pl.semaphore_signal(barrier, inc=1, device_id=partner, device_id_type=MESH)
+    pl.semaphore_wait(barrier, 3)
+    sent, written = [], []
+
+    def prepare(chunk):
+        start, count = chunks[chunk]
+        for part in range(4):
+            for frame in range(local):
+                first = part * share + start
+                some = max(min(count, slots - first), 0)
+                if some > 0:
+                    unit, _ = norm_parts(video_ref[frame, first : first + some, :].astype(F32))
+                    normed[part, frame, start : start + some, :] = (unit * gain_ref[...] + shift_ref[...]).astype(BF16)
+                if some < count:
+                    normed[part, frame, start + some : start + count, :] = jnp.zeros((count - some, width), BF16)
+        for frame in range(local):
+            xs[me * local + frame, start : start + count, :] = normed[me, frame, start : start + count, :]
+
+    def move(chunk, distance, arriving=False):
+        start, count = chunks[chunk]
+        target = (me + distance) % 4
+        source = (me + 4 - distance) % 4 if arriving else me
+        return pltpu.make_async_remote_copy(
+            src_ref=normed.at[target, :, pl.ds(start, count)],
+            dst_ref=xs.at[pl.ds(source * local, local), pl.ds(start, count)],
+            send_sem=send_sem.at[chunk, distance], recv_sem=recv_sem.at[chunk, source],
+            device_id={"mp": target}, device_id_type=MESH,
+        )
+
+    def send(chunk):
+        for distance in (2, 3, 1):
+            copy = move(chunk, distance)
+            copy.start()
+            sent.append(copy)
+
+    def write(source, target):
+        copy = pltpu.make_async_copy(source, target, out_sem.at[len(written)])
+        copy.start()
+        written.append(copy)
+
+    rows = frames * STEP
+    row = lax.broadcasted_iota(jnp.int32, (rows, rows), 0)
+    col = lax.broadcasted_iota(jnp.int32, (rows, rows), 1)
+    same = row % STEP == col % STEP
+
+    def compute(chunk):
+        start, count = chunks[chunk]
+        span = pl.ds(start, count)
+        x = xs[:, start : start + count, :].reshape(frames * count, width)
+        shape = (frames, count, WIDE)
+        for group in range(groups):
+            lanes = slice(group * WIDE, (group + 1) * WIDE)
+            part = lambda place: slice(place * width + group * WIDE, place * width + (group + 1) * WIDE)
+            q = (dot(x, w_ref[:, part(0)]) + bias_ref[:, part(0)]) * HEAD_DIM**-0.5
+            v = dot(x, w_ref[:, part(2)]) + bias_ref[:, part(1)]
+            qs[:, start : start + count, lanes] = q.astype(BF16).reshape(shape)
+            ks[:, start : start + count, lanes] = dot(x, w_ref[:, part(1)]).astype(BF16).reshape(shape)
+            vs[:, start : start + count, lanes] = v.astype(BF16).reshape(shape)
+            for step in range(start // STEP, (start + count) // STEP):
+                block = slice(step * STEP, (step + 1) * STEP)
+                keys = stacked(ks[:, block, lanes].reshape(rows, WIDE), rows)
+                values = stacked(vs[:, block, lanes].reshape(rows, WIDE), rows)
+                scores = dot_nt(qs[:, block, lanes].reshape(rows, WIDE), keys)
+                mixing = []
+                for head in range(GROUP):
+                    s = jnp.where(same, scores[:, head * rows : (head + 1) * rows], -1e30)
+                    e = jnp.exp(s - jnp.max(s, axis=1, keepdims=True))
+                    mixing.append((e / jnp.sum(e, axis=1, keepdims=True)).astype(BF16))
+                o = dot(jnp.concatenate(mixing, axis=1), values).astype(BF16).reshape(4, local, STEP, WIDE)
+                for frame in range(local):
+                    os[frame, :, block, lanes] = o[:, frame]
+        for frame in range(local):
+            write(os.at[frame, :, span], o_outs[frame].at[:, span])
+        for held, out in ((xs, x_out), (qs, q_out), (ks, k_out), (vs, v_out)):
+            write(held.at[:, span], out.at[:, span])
+
+    for chunk in range(len(chunks)):
+        prepare(chunk)
+        if chunk < 2:
+            send(chunk)
+    for chunk in range(len(chunks)):
+        for distance in (1, 2, 3):
+            move(chunk, distance, True).wait_recv()
+        if chunk + 2 < len(chunks):
+            send(chunk + 2)
+        compute(chunk)
+    for copy in sent:
+        copy.wait_send()
+    for copy in written:
+        copy.wait()
+
+
+def temporal_head(video, gain, shift, weight, bias, share, number):
+    local, slots, width = video.shape
+    frames = 4 * local
+    blocks = share // STEP
+    count = 4
+    chunks, at = [], 0
+    for i in range(count):
+        size = (blocks // count + (1 if i < blocks % count else 0)) * STEP
+        chunks.append((at, size))
+        at += size
+    whole = pl.BlockSpec(memory_space=pltpu.VMEM)
+    anywhere = pl.BlockSpec(memory_space=pl.ANY)
+    by_position = (frames, share, width)
+    return pl.pallas_call(
+        functools.partial(temporal_head_body, chunks=chunks, local=local),
+        in_specs=[whole] * 5,
+        out_specs=[anywhere] * (4 + local),
+        out_shape=[jax.ShapeDtypeStruct(by_position, BF16)] * 4 + [jax.ShapeDtypeStruct((4, share, width), BF16)] * local,
+        scratch_shapes=[pltpu.VMEM((4, local, share, width), BF16)] + [pltpu.VMEM(by_position, BF16)] * 4
+        + [pltpu.VMEM((local, 4, share, width), BF16)]
+        + [pltpu.SemaphoreType.DMA((count, 4))] * 2 + [pltpu.SemaphoreType.DMA((count * (4 + local),))],
+        cost_estimate=pl.CostEstimate(flops=70 * 10**9, bytes_accessed=20 * MIB, transcendentals=0),
+        compiler_params=pltpu.CompilerParams(vmem_limit_bytes=56 * MIB, collective_id=number, has_side_effects=True),
+        name="temporal_head",
+    )(video, gain, shift, weight, bias)
+
+
 def middle_and_space(frame, mixed, video, proj, proj_bias, gain, shift, weight, bias, patch_width):
     first, normed, qkv = middle(frame, mixed, video, proj, proj_bias, gain, shift, weight, bias)
     space_mixed, lse = spatial_fwd(patch_width, qkv, 1, video.shape[1])
@@ -1113,11 +1243,14 @@
 
     by_position = lambda value: value.reshape(parts * frames, share, width)
     by_device = lambda value: value.reshape(parts, frames, share, width)
-    normed_in = norm_in(video, temporal_gain, temporal_shift, parts, share)
-    x = by_position(exchange(normed_in))
-    own, x = lax.optimization_barrier((own, x))
     column = lax.all_gather(own, "mp", axis=0, tiled=True)
-    tq, tk, tv, *time_mixed = temporal_fwd(x, temporal_qkv, row(temporal_qv_bias), frames)
+    if reducible(width, planes, parts):
+        x, tq, tk, tv, *time_mixed = temporal_head(
+            video, temporal_gain, temporal_shift, temporal_qkv, row(temporal_qv_bias), share, 2
+        )
+    else:
+        x = by_position(exchange(norm_in(video, temporal_gain, temporal_shift, parts, share)))
+        tq, tk, tv, *time_mixed = temporal_fwd(x, temporal_qkv, row(temporal_qv_bias), frames)
     column, *time_mixed = lax.optimization_barrier((column, *time_mixed))
     fb1 = column[:, piece : piece + 1, :units].astype(F32)
     joint = lax.all_gather(column[:, :piece], "dp", axis=1, tiled=True)

time: 592 us -> 587 us (level)
  waiting for transfers between devices: 91.1 us -> 30.6 us
  Pallas kernels: 440 us -> 498 us
    pallas_call x2 -> x1, Pallas kernels: 32.5 us -> 91 us  [temporal_head(): pl.pallas_call(functools.partial(temporal_head_body, chunks=chunks, local...]
    all_to_all x5 -> x4, waiting for transfers between devices: 86.4 us -> 30.5 us  [exchange(): return lax.all_to_all(value, 'mp', split_axis=0, concat_axis=0, tiled=True)]
    all_to_all x5 -> x4, starting transfers between devices: 22.3 us -> 17.6 us  [exchange(): return lax.all_to_all(value, 'mp', split_axis=0, concat_axis=0, tiled=True)]
  transfers between devices with their start and end apart: 9 -> 8, of which waited for: 4 -> 3; matrix products, arithmetic and copies ran while one was open for 1% -> 1% of each run, Pallas kernels for 62% -> 73%
where the time goes in v1:
time: 587 us; the launch traced here: 576 us
  Pallas kernels  498 us (85%)
  waiting for transfers between devices  30.6 us (5%)
  starting transfers between devices  17.8 us (3%)
  between operations  14.9 us (3%)
  local copies, waits for them, and re-layouts  10.4 us (2%)
    pallas_call x1, Pallas kernels, temporal_tail(): pl.pallas_call(functools.partial(temporal_tail_body, planes=planes, early...  146 us
    pallas_call x1, Pallas kernels, temporal_head(): pl.pallas_call(functools.partial(temporal_head_body, chunks=chunks, local...  91 us
    pallas_call x2, Pallas kernels, spatial_bwd(): pl.pallas_call(functools.partial(spatial_bwd_body, slots=slots, rows=rows...  57.4 us
    pallas_call x1, Pallas kernels, feed(): pl.pallas_call(functools.partial(feed_body, sub=sub, frames=frames), grid...  51.8 us
    pallas_call x2, Pallas kernels, spatial_fwd(): pl.pallas_call(functools.partial(spatial_fwd_body, slots=slots, rows=rows...  34.5 us
    all_to_all x4, waiting for transfers between devices, exchange(): return lax.all_to_all(value, 'mp', split_axis=0, concat_axis=0, tiled=True)  30.5 us
    pallas_call x5, Pallas kernels, weight_grad(): pl.pallas_call(tn_body, grid=(width // WIDE,), in_specs=[fixed(value.shap...  30.4 us
    pallas_call x2, Pallas kernels, middle_bwd(): pl.pallas_call(middle_bwd_body, grid=(1,), in_specs=[fixed((slots, width)...  25.8 us
  transfers between devices with their start and end apart: 8, of which 3 were waited for; matrix products, arithmetic and copies ran while one was open for 1% of the time, Pallas kernels for 73%

profile of v1, /device:TPU:0, one launch (start us, length us, event | category | flops | bytes accessed | tf_op | source)
XLA Modules:
  0.0 576.5 jit_solution(17940604822696497365)
XLA Ops:
  7.3 1.7 copy.52
  10.4 91.0 %temporal_head.1 = (bf16[8,208,768]{2,1,0:T(8,128)(2,1)}, bf16[8,208,768]{2,1,0:T(8,128)(2,1)}, bf16[8,208,768]{2,1,0:T(8,128)(2,1)}, bf16[8,208,768]{2,1,0:T(8,...) custom-call(bf16[2,784,768]{2,1,0:T(8,128)(2,1)} %bitcast.36, f32[768]{0:T(1024)} %gain_ref.15, ...), custom_call_target="tpu_custom_call" | custom-call | flops 70000001024 | bytes 20971520 | tf_op jit(solution)/shard_map/temporal_head/pallas_call | solution.py:1184
  101.4 2.4 slice.63
  103.8 6.5 %all-to-all-start = ((bf16[4,208,768]{2,1,0:T(8,128)(2,1)}), bf16[4,208,768]{2,1,0:T(8,128)(2,1)S(1)}, u32[]{:S(2)}, u32[]{:S(2)}) async-start(bf16[4,208,768]{2,1,0:T(8,128)(2,1)} %get-tuple-element.80), calls=%async_computation | async-start | bytes 2555904 | tf_op jit(solution)/shard_map/all_to_all | solution.py:1242
  111.6 1.4 slice_convert_fusion.fb1_ref
  113.0 26.7 %all-to-all-done.mixed_ref.refs_0_ = bf16[4,208,768]{2,1,0:T(8,128)(2,1)S(1)} async-done(((bf16[4,208,768]{2,1,0:T(8,128)(2,1)}), bf16[4,208,768]{2,1,0:T(8,128)(2,1)S(1)}, u32[]{:S(2)}, u32[]{:S(2)}) %all-to-all-start) | async-done | bytes 1277984 | tf_op jit(solution)/shard_map/all_to_all | solution.py:1242
  139.7 3.5 all-to-all-start.1
  143.3 10.1 %middle.2 = (f32[784,768]{1,0:T(8,128)}, bf16[784,768]{1,0:T(8,128)(2,1)}, bf16[784,2304]{1,0:T(8,128)(2,1)}) custom-call(bf16[4,208,768]{2,1,0:T(8,128)(2,1)} %copy-done, bf16[2,784,768]{2,1,0:T(8,128)(2,1)} %bitcast.37, bf16[768,768]{1,0:T(8,128)(2,1)} %proj_ref.9, f32[768]{0:T(1024)} %pb_ref.4, f32[768]{0:T(1024)} %gain_ref.13, f32[768]{0:T(1024)} %shift_ref.7, ...), custom_call_target="tpu_custom_call" | custom-call | flops 11000000512 | bytes 14680064 | tf_op jit(solution)/shard_map/middle/pallas_call | solution.py:406
  153.3 17.3 %spatial_fwd.2 = (bf16[1,784,768]{2,1,0:T(8,128)(2,1)}, f32[1,3,8,784]{3,2,1,0:T(8,128)}) custom-call(s32[1]{0:T(128)S(6)} %copy.56.width_ref, bf16[1,784,2304]{2,1,0:T(8,128)(2,1)} %bitcast.56, bf16[1,784,2304]{2,1,0:T(8,128)(2,1)} %bitcast.57, bf16[1,784,2304]{2,1,0:T(8,128)(2,1)} %bitcast.58), custom_call_target="tpu_custom_call" | custom-call | flops 20000000000 | bytes 5242880 | tf_op jit(solution)/shard_map/spatial_fwd/pallas_call | solution.py:95
  170.7 2.7 all-to-all-done.1.mixed_ref.refs_1_
  173.3 1.0 copy-done.1
  174.4 9.9 %middle.3 = (f32[784,768]{1,0:T(8,128)}, bf16[784,768]{1,0:T(8,128)(2,1)}, bf16[784,2304]{1,0:T(8,128)(2,1)}) custom-call(bf16[4,208,768]{2,1,0:T(8,128)(2,1)} %copy-done.1, bf16[2,784,768]{2,1,0:T(8,128)(2,1)} %bitcast.38, bf16[768,768]{1,0:T(8,128)(2,1)} %proj_ref.9, f32[768]{0:T(1024)} %pb_ref.4, f32[768]{0:T(1024)} %gain_ref.13, f32[768]{0:T(1024)} %shift_ref.7, ...), custom_call_target="tpu_custom_call" | custom-call | flops 11000000512 | bytes 14680064 | tf_op jit(solution)/shard_map/middle/pallas_call | solution.py:406
  184.3 17.2 %spatial_fwd.3 = (bf16[1,784,768]{2,1,0:T(8,128)(2,1)}, f32[1,3,8,784]{3,2,1,0:T(8,128)}) custom-call(s32[1]{0:T(128)S(6)} %copy.56.width_ref, bf16[1,784,2304]{2,1,0:T(8,128)(2,1)} %bitcast.50, bf16[1,784,2304]{2,1,0:T(8,128)(2,1)} %bitcast.51, bf16[1,784,2304]{2,1,0:T(8,128)(2,1)} %bitcast.52), custom_call_target="tpu_custom_call" | custom-call | flops 20000000000 | bytes 5242880 | tf_op jit(solution)/shard_map/spatial_fwd/pallas_call | solution.py:95
  201.4 51.8 %feed.1 = (bf16[2,784,768]{2,1,0:T(8,128)(2,1)}, bf16[2,784,768]{2,1,0:T(8,128)(2,1)}, bf16[4,2,784,768]{3,2,1,0:T(8,128)(2,1)}, bf16[4,2,784,768]{3,2,1,0:T(8,1...) custom-call(bf16[2,784,768]{2,1,0:T(8,128)(2,1)} %bitcast.46, ...), custom_call_target="tpu_custom_call" | custom-call | flops 56000000000 | bytes 62914560 | tf_op jit(solution)/shard_map/feed/pallas_call | solution.py:497
  253.2 23.1 %fc_grads.1 = bf16[4,768,1536]{2,1,0:T(8,128)(2,1)} custom-call(bf16[1568,768]{1,0:T(8,128)(2,1)} %bitcast.63, bf16[1568,768]{1,0:T(8,128)(2,1)} %bitcast.47, bf16[4,1568,768]{2,1,0:T(8,128)(2,1)} %bitcast.49, bf16[4,1568,768]{2,1,0:T(8,128)(2,1)} %bitcast.48), custom_call_target="tpu_custom_call" | custom-call | flops 14797504512 | bytes 19267584 | tf_op jit(solution)/shard_map/fc_grads/pallas_call | solution.py:628
  276.3 28.5 %spatial_bwd.2 = (bf16[1,784,768]{2,1,0:T(8,128)(2,1)}, bf16[1,784,768]{2,1,0:T(8,128)(2,1)}, bf16[1,784,768]{2,1,0:T(8,128)(2,1)}) custom-call(s32[1]{0:T(128)S(6)} %copy.56.width_ref, bf16[1,784,2304]{2,1,0:T(8,128)(2,1)} %bitcast.59, bf16[1,784,2304]{2,1,0:T(8,128)(2,1)} %bitcast.60, bf16[1,784,2304]{2,1,0:T(8,128)(2,1)} %bitcast.61, ...), custom_call_target="tpu_custom_call" | custom-call | flops 32000000000 | bytes 9437184 | tf_op jit(solution)/shard_map/spatial_bwd/pallas_call | solution.py:175
  304.9 12.8 %middle_bwd.2 = (f32[784,768]{1,0:T(8,128)}, bf16[784,768]{1,0:T(8,128)(2,1)}, bf16[4,208,768]{2,1,0:T(8,128)(2,1)}, f32[8,768]{1,0:T(8,128)}) custom-call(bf16[784,768]{1,0:T(8,128)(2,1)} %bitcast.64, bf16[784,768]{1,0:T(8,128)(2,1)} %bitcast.66, bf16[784,768]{1,0:T(8,128)(2,1)} %bitcast.68, bf16[768,2304]{1,0:T(8,128)(2,1)} %w_ref.9, ...), custom_call_target="tpu_custom_call" | custom-call | flops 14000000000 | bytes 16777216 | tf_op jit(solution)/shard_map/middle_bwd/pallas_call | solution.py:537
  317.7 3.6 all-to-all-start.2
  321.3 28.9 %spatial_bwd.3 = (bf16[1,784,768]{2,1,0:T(8,128)(2,1)}, bf16[1,784,768]{2,1,0:T(8,128)(2,1)}, bf16[1,784,768]{2,1,0:T(8,128)(2,1)}) custom-call(s32[1]{0:T(128)S(6)} %copy.56.width_ref, bf16[1,784,2304]{2,1,0:T(8,128)(2,1)} %bitcast.53, bf16[1,784,2304]{2,1,0:T(8,128)(2,1)} %bitcast.54, bf16[1,784,2304]{2,1,0:T(8,128)(2,1)} %bitcast.55, ...), custom_call_target="tpu_custom_call" | custom-call | flops 32000000000 | bytes 9437184 | tf_op jit(solution)/shard_map/spatial_bwd/pallas_call | solution.py:175
  350.1 1.2 all-to-all-done.2.refs_0_
  351.3 13.0 %middle_bwd.3 = (f32[784,768]{1,0:T(8,128)}, bf16[784,768]{1,0:T(8,128)(2,1)}, bf16[4,208,768]{2,1,0:T(8,128)(2,1)}, f32[8,768]{1,0:T(8,128)}) custom-call(bf16[784,768]{1,0:T(8,128)(2,1)} %bitcast.70, bf16[784,768]{1,0:T(8,128)(2,1)} %bitcast.72, bf16[784,768]{1,0:T(8,128)(2,1)} %bitcast.74, bf16[768,2304]{1,0:T(8,128)(2,1)} %w_ref.9, ...), custom_call_target="tpu_custom_call" | custom-call | flops 14000000000 | bytes 16777216 | tf_op jit(solution)/shard_map/middle_bwd/pallas_call | solution.py:537
  364.3 4.0 all-to-all-start.3
  368.5 6.0 %weight_grad.7.refs_9_ = bf16[768,768]{1,0:T(8,128)(2,1)} custom-call(bf16[784,768]{1,0:T(8,128)(2,1)} %get-tuple-element.115.refs_0_, bf16[784,768]{1,0:T(8,128)(2,1)} %get-tuple-element.116.refs_1_, bf16[784,768]{1,0:T(8,128)(2,1)} %bitcast.69, bf16[784,768]{1,0:T(8,128)(2,1)} %bitcast.75), custom_call_target="tpu_custom_call" | custom-call | flops 1849688064 | bytes 4816896 | tf_op jit(solution)/shard_map/weight_grad/pallas_call | solution.py:602
  374.5 6.1 %weight_grad.6.refs_8_ = bf16[768,768]{1,0:T(8,128)(2,1)} custom-call(bf16[784,768]{1,0:T(8,128)(2,1)} %get-tuple-element.115.refs_0_, bf16[784,768]{1,0:T(8,128)(2,1)} %get-tuple-element.116.refs_1_, bf16[784,768]{1,0:T(8,128)(2,1)} %bitcast.67, bf16[784,768]{1,0:T(8,128)(2,1)} %bitcast.73), custom_call_target="tpu_custom_call" | custom-call | flops 1849688064 | bytes 4816896 | tf_op jit(solution)/shard_map/weight_grad/pallas_call | solution.py:602
  380.6 6.0 %weight_grad.8.refs_10_ = bf16[768,768]{1,0:T(8,128)(2,1)} custom-call(bf16[784,768]{1,0:T(8,128)(2,1)} %bitcast.41, bf16[784,768]{1,0:T(8,128)(2,1)} %bitcast.43, bf16[1568,768]{1,0:T(8,128)(2,1)} %bitcast.32, bf16[1568,768]{1,0:T(8,128)(2,1)} %bitcast.33), custom_call_target="tpu_custom_call" | custom-call | flops 1849688064 | bytes 4816896 | tf_op jit(solution)/shard_map/weight_grad/pallas_call | solution.py:602
  386.6 6.0 %weight_grad.5.refs_7_ = bf16[768,768]{1,0:T(8,128)(2,1)} custom-call(bf16[784,768]{1,0:T(8,128)(2,1)} %get-tuple-element.115.refs_0_, bf16[784,768]{1,0:T(8,128)(2,1)} %get-tuple-element.116.refs_1_, bf16[784,768]{1,0:T(8,128)(2,1)} %bitcast.65, bf16[784,768]{1,0:T(8,128)(2,1)} %bitcast.71), custom_call_target="tpu_custom_call" | custom-call | flops 1849688064 | bytes 4816896 | tf_op jit(solution)/shard_map/weight_grad/pallas_call | solution.py:602
  392.6 6.3 %weight_grad.9.refs_11_ = bf16[768,768]{1,0:T(8,128)(2,1)} custom-call(bf16[4,208,768]{2,1,0:T(8,128)(2,1)} %copy-done, bf16[4,208,768]{2,1,0:T(8,128)(2,1)} %copy-done.1, bf16[784,768]{1,0:T(8,128)(2,1)} %get-tuple-element.118.refs_2_, bf16[784,768]{1,0:T(8,128)(2,1)} %get-tuple-element.119.refs_3_), custom_call_target="tpu_custom_call" | custom-call | flops 1849688064 | bytes 4816896 | tf_op jit(solution)/shard_map/weight_grad/pallas_call | solution.py:602
  399.7 1.0 copy-done.3
  400.7 146.0 %temporal_tail.1 = (bf16[4,2,208,768]{3,2,1,0:T(8,128)(2,1)}, bf16[8,768,768]{2,1,0:T(8,128)(2,1)}, f32[24,768]{1,0:T(8,128)}) custom-call(f32[768]{0:T(1024)} %gain_ref.15, f32[768]{0:T(1024)} %shift_ref.9, f32[24,768]{1,0:T(8,128)} %maximum_maximum_fusion.small_in, bf16[4,208,768]{2,1,0:T(8,128)(2,1)} %copy-done.2, bf16[4,208,768]{2,1,0:T(8,128)(2,1)} %copy-done.3, ...), custom_call_target="tpu_custom_call" | custom-call | flops 23555211264 | bytes 62914560 | tf_op jit(solution)/shard_map/temporal_tail/pallas_call | solution.py:1044
  548.1 10.3 %finish.1 = (f32[768,2304]{1,0:T(8,128)}, f32[768,2304]{1,0:T(8,128)}, f32[768,768]{1,0:T(8,128)}, f32[768,768]{1,0:T(8,128)}) custom-call(bf16[8,768,768]{2,1,0:T(8,128)(2,1)} %get-tuple-element.128.time_ref.space_ref.space_proj_ref.time_proj_ref, bf16[8,768,768]{2,1,0:T(8,128)(2,1)} %get-tuple-element.128.time_ref.space_ref.space_proj_ref.time_proj_ref, ...), custom_call_target="tpu_custom_call" | custom-call | flops 1000000000 | bytes 31457280 | tf_op jit(solution)/shard_map/finish/pallas_call | solution.py:660
  559.8 8.1 %norm_out.1 = f32[2,784,768]{2,1,0:T(8,128)} custom-call(bf16[4,2,208,768]{3,2,1,0:T(8,128)(2,1)} %get-tuple-element.120.grad_ref, bf16[2,784,768]{2,1,0:T(8,128)(2,1)} %bitcast.39, f32[768]{0:T(1024)} %gain_ref.15, f32[784,768]{1,0:T(8,128)} %get-tuple-element.121.refs_0_, f32[784,768]{1,0:T(8,128)} %get-tuple-element.126.refs_1_), custom_call_target="tpu_custom_call" | custom-call | flops 1000000000 | bytes 26214400 | tf_op jit(solution)/shard_map/norm_out/pallas_call | solution.py:571
  567.9 1.0 bitcast_convert_fusion
  (54 shorter events, 6.6 us)
Async XLA Ops:
  7.2 1.7 copy-start.12
  7.2 1.8 copy-start.4
  7.2 94.2 %all-gather.6.cloned.1.call-start = ((), (), s32[]{:S(2)}) async-start(), calls=%async_computation.9 | async-start | bytes 1720320 | tf_op jit(solution)/shard_map/all_gather | solution.py:1246
  9.0 0.9 copy-start.9
  9.8 191.7 %all-gather.4.cloned.1.call-start = ((), (), s32[]{:S(2)}) async-start(), calls=%async_computation.6 | async-start | bytes 10616832 | tf_op jit(solution)/shard_map/all_gather | solution.py:1256
  103.8 6.5 %copy-start.10 = (f32[1536]{0:T(1024)S(1)}, f32[1536]{0:T(1024)}, u32[]{:S(2)}) copy-start(f32[1536]{0:T(1024)} %param.32) | copy-start | bytes 18436
  103.8 35.8 %all-to-all-start = ((bf16[4,208,768]{2,1,0:T(8,128)(2,1)}), bf16[4,208,768]{2,1,0:T(8,128)(2,1)S(1)}, u32[]{:S(2)}, u32[]{:S(2)}) async-start(bf16[4,208,768]{2,1,0:T(8,128)(2,1)} %get-tuple-element.80), calls=%async_computation | async-start | bytes 2555904 | tf_op jit(solution)/shard_map/all_to_all | solution.py:1242
  139.7 3.6 copy-start
  139.7 33.6 %all-to-all-start.1 = ((bf16[4,208,768]{2,1,0:T(8,128)(2,1)}), bf16[4,208,768]{2,1,0:T(8,128)(2,1)S(1)}, u32[]{:S(2)}, u32[]{:S(2)}) async-start(bf16[4,208,768]{2,1,0:T(8,128)(2,1)} %get-tuple-element.82), calls=%async_computation.1 | async-start | bytes 2555904 | tf_op jit(solution)/shard_map/all_to_all | solution.py:1242
  143.2 256.4 %reduce-scatter.3.cloned.1.call-start = ((), (), s32[]{:S(2)}) async-start(), calls=%async_computation.7 | async-start | bytes 10616832 | tf_op jit(solution)/shard_map/reduce_scatter | solution.py:1277
  173.3 1.0 copy-start.1
  317.7 33.6 %all-to-all-start.2 = ((bf16[4,208,768]{2,1,0:T(8,128)(2,1)}), bf16[4,208,768]{2,1,0:T(8,128)(2,1)S(1)}, u32[]{:S(2)}, u32[]{:S(2)}) async-start(bf16[4,208,768]{2,1,0:T(8,128)(2,1)} %get-tuple-element.101), calls=%async_computation.2 | async-start | bytes 2555904 | tf_op jit(solution)/shard_map/all_to_all | solution.py:1242
  351.3 13.0 %copy-start.2 = (bf16[4,208,768]{2,1,0:T(8,128)(2,1)}, bf16[4,208,768]{2,1,0:T(8,128)(2,1)S(1)}, u32[]{:S(2)}) copy-start(bf16[4,208,768]{2,1,0:T(8,128)(2,1)S(1)} %all-to-all-done.2.refs_0_) | copy-start | bytes 3833860
  364.3 4.1 copy-start.5
  364.3 4.2 copy-start.11
  364.3 35.3 %all-to-all-start.3 = ((bf16[4,208,768]{2,1,0:T(8,128)(2,1)}), bf16[4,208,768]{2,1,0:T(8,128)(2,1)S(1)}, u32[]{:S(2)}, u32[]{:S(2)}) async-start(bf16[4,208,768]{2,1,0:T(8,128)(2,1)} %get-tuple-element.110), calls=%async_computation.3 | async-start | bytes 2555904 | tf_op jit(solution)/shard_map/all_to_all | solution.py:1242
  368.4 199.5 %reduce-scatter.5.cloned.1.call-start = ((), (), s32[]{:S(2)}) async-start(), calls=%async_computation.8 | async-start | bytes 1474560 | tf_op jit(solution)/shard_map/reduce_scatter | solution.py:1302
  392.6 6.3 %copy-start.7 = (f32[8,768]{1,0:T(8,128)S(1)}, f32[8,768]{1,0:T(8,128)}, u32[]{:S(2)}) copy-start(f32[8,768]{1,0:T(8,128)} %get-tuple-element.99) | copy-start | bytes 73732
  392.6 6.3 %copy-start.8 = (f32[8,768]{1,0:T(8,128)S(1)}, f32[8,768]{1,0:T(8,128)}, u32[]{:S(2)}) copy-start(f32[8,768]{1,0:T(8,128)} %get-tuple-element.108) | copy-start | bytes 73732
  399.7 1.0 copy-start.3
  548.1 10.4 %copy-start.6 = (f32[24,768]{1,0:T(8,128)S(1)}, f32[24,768]{1,0:T(8,128)}, u32[]{:S(2)}) copy-start(f32[24,768]{1,0:T(8,128)} %get-tuple-element.127) | copy-start | bytes 221188
Sparse Core Ops, SparseCore 0:
  10.2 64.8 all-gather.5
  103.9 61.6 all-gather.3
  276.4 74.6 reduce-scatter.2
  399.8 33.0 reduce-scatter.4

commit v2 on v1

--- a/solution.py
+++ b/solution.py
@@ -675,6 +675,16 @@
 MESH = pl.DeviceIdType.MESH
 EARLY_GAP = 3.0
 HOP = 4.0
+RATE = 1
+
+
+def cuts_of(rows, count):
+    blocks, cuts, at = rows // 16, [], 0
+    for i in range(count):
+        size = (blocks // count + (1 if i < blocks % count else 0)) * 16
+        cuts.append((at, size))
+        at += size
+    return cuts
 
 
 def bits_of(count):
@@ -961,8 +971,7 @@
                     total = total + dot_nt(d[:, place * WIDE : (place + 1) * WIDE], weight)
             dx_ref[some] = total.astype(BF16).reshape(quarter, slots, width)
             if distance:
-                moves.append(move(distance))
-                moves[-1].start()
+                queue.extend((distance, cut) for cut in range(len(cuts)))
             else:
                 keep = pltpu.make_async_copy(dx_ref.at[some], moved_ref.at[ring.part], move_local.at[0])
                 keep.start()
@@ -974,15 +983,24 @@
         small_ref[taken + 2 : taken + 3, :] = (product - shift_ref[...][None] * shift_grad) / gain_ref[...][None]
         small_ref[taken + 3 : taken + 4, :] = shift_grad
 
-    moves, kept = [], []
-
-    def move(distance, arriving=False):
+    moves, kept, queue = [], [], []
+    cuts = cuts_of(slots, 4)
+
+    def move(distance, cut, arriving=False):
         target = (ring.part + distance) % 4
         source = (ring.part + 4 - distance) % 4 if arriving else ring.part
+        span = pl.ds(*cuts[cut])
         return pltpu.make_async_remote_copy(
-            src_ref=dx_ref.at[pl.ds(target * (frames // 4), frames // 4)], dst_ref=moved_ref.at[source],
-            send_sem=move_send.at[distance], recv_sem=move_recv.at[source], device_id={"mp": target}, device_id_type=MESH,
+            src_ref=dx_ref.at[pl.ds(target * (frames // 4), frames // 4), span], dst_ref=moved_ref.at[source, :, span],
+            send_sem=move_send.at[distance, cut], recv_sem=move_recv.at[source, cut],
+            device_id={"mp": target}, device_id_type=MESH,
         )
+
+    def send_some():
+        for _ in range(RATE):
+            if queue:
+                moves.append(move(*queue.pop(0)))
+                moves[-1].start()
 
     partners = [ring.by_bit[bit] for bit in ring.bits] + [ring.beside, ring.third]
     small_wait = []
@@ -1017,16 +1035,19 @@
     advance_all()
     for spent in compute():
         clock += spent
+        send_some()
         advance_all()
     small_at = 0
-    while any(step < sums.steps for step in following) or small_at <= len(partners):
+    while any(step < sums.steps for step in following) or small_at <= len(partners) or queue:
         clock += HOP
+        send_some()
         advance_all()
         if small_at <= len(partners):
             small_step(small_at)
             small_at += 1
     for distance in (1, 2, 3):
-        move(distance, True).wait_recv()
+        for cut in range(len(cuts)):
+            move(distance, cut, True).wait_recv()
     for copy in moves:
         copy.wait_send()
     kept[0].wait()
@@ -1055,7 +1076,7 @@
             pltpu.VMEM((groups, frames, slots, 3 * WIDE), BF16), pltpu.VMEM(x.shape, BF16),
             pltpu.VMEM((len(early) + groups, width, width), BF16),
             pltpu.SemaphoreType.DMA((len(early) + 2 + 3 * groups,)),
-            pltpu.SemaphoreType.DMA((4,)), pltpu.SemaphoreType.DMA((4,)), pltpu.SemaphoreType.DMA((1,)),
+            pltpu.SemaphoreType.DMA((4, 4)), pltpu.SemaphoreType.DMA((4, 4)), pltpu.SemaphoreType.DMA((1,)),
             pltpu.VMEM(small.shape, F32), pltpu.VMEM((deep + 2,) + small.shape, F32), pltpu.VMEM((deep + 1,) + small.shape, F32),
             pltpu.SemaphoreType.DMA((deep + 2,)), pltpu.SemaphoreType.DMA((deep + 2,)),
         ] + reduction_scratch(chains, width, deep),
@@ -1063,6 +1084,9 @@
         compiler_params=pltpu.CompilerParams(vmem_limit_bytes=62 * MIB, collective_id=number, has_side_effects=True),
         name="temporal_tail",
     )(gain, shift, small, *grad, x, q, k, v, weight, *early)
+
+
+AHEAD = 2
 
 
 def temporal_head_body(video_ref, gain_ref, shift_ref, w_ref, bias_ref, *refs, chunks, local):
@@ -1154,13 +1178,13 @@
 
     for chunk in range(len(chunks)):
         prepare(chunk)
-        if chunk < 2:
+        if chunk < AHEAD:
             send(chunk)
     for chunk in range(len(chunks)):
         for distance in (1, 2, 3):
             move(chunk, distance, True).wait_recv()
-        if chunk + 2 < len(chunks):
-            send(chunk + 2)
+        if chunk + AHEAD < len(chunks):
+            send(chunk + AHEAD)
         compute(chunk)
     for copy in sent:
         copy.wait_send()
@@ -1171,13 +1195,8 @@
 def temporal_head(video, gain, shift, weight, bias, share, number):
     local, slots, width = video.shape
     frames = 4 * local
-    blocks = share // STEP
     count = 4
-    chunks, at = [], 0
-    for i in range(count):
-        size = (blocks // count + (1 if i < blocks % count else 0)) * STEP
-        chunks.append((at, size))
-        at += size
+    chunks = cuts_of(share, count)
     whole = pl.BlockSpec(memory_space=pltpu.VMEM)
     anywhere = pl.BlockSpec(memory_space=pl.ANY)
     by_position = (frames, share, width)

time: 587 us -> 577 us (0.983)
  Pallas kernels: 498 us -> 475 us
  waiting for transfers between devices: 30.6 us -> 43.9 us
    pallas_call x2, Pallas kernels: 57.4 us -> 41.7 us  [spatial_bwd(): pl.pallas_call(functools.partial(spatial_bwd_body, slots=slots, rows=rows...]
    all_to_all x4, waiting for transfers between devices: 30.5 us -> 43.8 us  [exchange(): return lax.all_to_all(value, 'mp', split_axis=0, concat_axis=0, tiled=True)]
    pallas_call x2, Pallas kernels: 34.5 us -> 24.1 us  [spatial_fwd(): pl.pallas_call(functools.partial(spatial_fwd_body, slots=slots, rows=rows...]
  transfers between devices with their start and end apart: 8 -> 8, of which waited for: 3 -> 3; matrix products, arithmetic and copies ran while one was open for 1% -> 1% of each run, Pallas kernels for 73% -> 71%
where the time goes in v2:
time: 577 us; the launch traced here: 566 us
  Pallas kernels  475 us (82%)
  waiting for transfers between devices  43.9 us (8%)
  starting transfers between devices  17.4 us (3%)
  between operations  14.9 us (3%)
  local copies, waits for them, and re-layouts  10.4 us (2%)
    pallas_call x1, Pallas kernels, temporal_tail(): pl.pallas_call(functools.partial(temporal_tail_body, planes=planes, early...  149 us
    pallas_call x1, Pallas kernels, temporal_head(): pl.pallas_call(functools.partial(temporal_head_body, chunks=chunks, local...  91 us
    pallas_call x1, Pallas kernels, feed(): pl.pallas_call(functools.partial(feed_body, sub=sub, frames=frames), grid...  51.8 us
    all_to_all x4, waiting for transfers between devices, exchange(): return lax.all_to_all(value, 'mp', split_axis=0, concat_axis=0, tiled=True)  43.8 us
    pallas_call x2, Pallas kernels, spatial_bwd(): pl.pallas_call(functools.partial(spatial_bwd_body, slots=slots, rows=rows...  41.7 us
    pallas_call x5, Pallas kernels, weight_grad(): pl.pallas_call(tn_body, grid=(width // WIDE,), in_specs=[fixed(value.shap...  30.4 us
    pallas_call x2, Pallas kernels, middle_bwd(): pl.pallas_call(middle_bwd_body, grid=(1,), in_specs=[fixed((slots, width)...  25.9 us
    pallas_call x2, Pallas kernels, spatial_fwd(): pl.pallas_call(functools.partial(spatial_fwd_body, slots=slots, rows=rows...  24.1 us
  transfers between devices with their start and end apart: 8, of which 3 were waited for; matrix products, arithmetic and copies ran while one was open for 1% of the time, Pallas kernels for 71%

profile of v2, /device:TPU:0, one launch (start us, length us, event | category | flops | bytes accessed | tf_op | source)
XLA Modules:
  0.0 566.1 jit_solution(6668591438839270926)
XLA Ops:
  7.3 1.7 copy.52
  10.4 91.0 %temporal_head.1 = (bf16[8,208,768]{2,1,0:T(8,128)(2,1)}, bf16[8,208,768]{2,1,0:T(8,128)(2,1)}, bf16[8,208,768]{2,1,0:T(8,128)(2,1)}, bf16[8,208,768]{2,1,0:T(8,...) custom-call(bf16[2,784,768]{2,1,0:T(8,128)(2,1)} %bitcast.36, f32[768]{0:T(1024)} %gain_ref.15, ...), custom_call_target="tpu_custom_call" | custom-call | flops 70000001024 | bytes 20971520 | tf_op jit(solution)/shard_map/temporal_head/pallas_call | solution.py:1203
  101.4 2.4 slice.63
  103.8 6.5 %all-to-all-start = ((bf16[4,208,768]{2,1,0:T(8,128)(2,1)}), bf16[4,208,768]{2,1,0:T(8,128)(2,1)S(1)}, u32[]{:S(2)}, u32[]{:S(2)}) async-start(bf16[4,208,768]{2,1,0:T(8,128)(2,1)} %get-tuple-element.80), calls=%async_computation | async-start | bytes 2555904 | tf_op jit(solution)/shard_map/all_to_all | solution.py:1261
  111.6 1.4 slice_convert_fusion.fb1_ref
  113.0 26.7 %all-to-all-done.mixed_ref.refs_0_ = bf16[4,208,768]{2,1,0:T(8,128)(2,1)S(1)} async-done(((bf16[4,208,768]{2,1,0:T(8,128)(2,1)}), bf16[4,208,768]{2,1,0:T(8,128)(2,1)S(1)}, u32[]{:S(2)}, u32[]{:S(2)}) %all-to-all-start) | async-done | bytes 1277984 | tf_op jit(solution)/shard_map/all_to_all | solution.py:1261
  139.7 3.5 all-to-all-start.1
  143.3 10.1 %middle.2 = (f32[784,768]{1,0:T(8,128)}, bf16[784,768]{1,0:T(8,128)(2,1)}, bf16[784,2304]{1,0:T(8,128)(2,1)}) custom-call(bf16[4,208,768]{2,1,0:T(8,128)(2,1)} %copy-done, bf16[2,784,768]{2,1,0:T(8,128)(2,1)} %bitcast.37, bf16[768,768]{1,0:T(8,128)(2,1)} %proj_ref.9, f32[768]{0:T(1024)} %pb_ref.4, f32[768]{0:T(1024)} %gain_ref.13, f32[768]{0:T(1024)} %shift_ref.7, ...), custom_call_target="tpu_custom_call" | custom-call | flops 11000000512 | bytes 14680064 | tf_op jit(solution)/shard_map/middle/pallas_call | solution.py:406
  153.3 12.1 %spatial_fwd.2 = (bf16[1,784,768]{2,1,0:T(8,128)(2,1)}, f32[1,3,8,784]{3,2,1,0:T(8,128)}) custom-call(s32[1]{0:T(128)S(6)} %copy.56.width_ref, bf16[1,784,2304]{2,1,0:T(8,128)(2,1)} %bitcast.56, bf16[1,784,2304]{2,1,0:T(8,128)(2,1)} %bitcast.57, bf16[1,784,2304]{2,1,0:T(8,128)(2,1)} %bitcast.58), custom_call_target="tpu_custom_call" | custom-call | flops 20000000000 | bytes 5242880 | tf_op jit(solution)/shard_map/spatial_fwd/pallas_call | solution.py:95
  165.5 7.8 %all-to-all-done.1.mixed_ref.refs_1_ = bf16[4,208,768]{2,1,0:T(8,128)(2,1)S(1)} async-done(((bf16[4,208,768]{2,1,0:T(8,128)(2,1)}), bf16[4,208,768]{2,1,0:T(8,128)(2,1)S(1)}, u32[]{:S(2)}, u32[]{:S(2)}) %all-to-all-start.1) | async-done | bytes 1277984 | tf_op jit(solution)/shard_map/all_to_all | solution.py:1261
  173.3 1.0 copy-done.1
  174.4 9.9 %middle.3 = (f32[784,768]{1,0:T(8,128)}, bf16[784,768]{1,0:T(8,128)(2,1)}, bf16[784,2304]{1,0:T(8,128)(2,1)}) custom-call(bf16[4,208,768]{2,1,0:T(8,128)(2,1)} %copy-done.1, bf16[2,784,768]{2,1,0:T(8,128)(2,1)} %bitcast.38, bf16[768,768]{1,0:T(8,128)(2,1)} %proj_ref.9, f32[768]{0:T(1024)} %pb_ref.4, f32[768]{0:T(1024)} %gain_ref.13, f32[768]{0:T(1024)} %shift_ref.7, ...), custom_call_target="tpu_custom_call" | custom-call | flops 11000000512 | bytes 14680064 | tf_op jit(solution)/shard_map/middle/pallas_call | solution.py:406
  184.3 12.0 %spatial_fwd.3 = (bf16[1,784,768]{2,1,0:T(8,128)(2,1)}, f32[1,3,8,784]{3,2,1,0:T(8,128)}) custom-call(s32[1]{0:T(128)S(6)} %copy.56.width_ref, bf16[1,784,2304]{2,1,0:T(8,128)(2,1)} %bitcast.50, bf16[1,784,2304]{2,1,0:T(8,128)(2,1)} %bitcast.51, bf16[1,784,2304]{2,1,0:T(8,128)(2,1)} %bitcast.52), custom_call_target="tpu_custom_call" | custom-call | flops 20000000000 | bytes 5242880 | tf_op jit(solution)/shard_map/spatial_fwd/pallas_call | solution.py:95
  196.3 51.8 %feed.1 = (bf16[2,784,768]{2,1,0:T(8,128)(2,1)}, bf16[2,784,768]{2,1,0:T(8,128)(2,1)}, bf16[4,2,784,768]{3,2,1,0:T(8,128)(2,1)}, bf16[4,2,784,768]{3,2,1,0:T(8,1...) custom-call(bf16[2,784,768]{2,1,0:T(8,128)(2,1)} %bitcast.46, ...), custom_call_target="tpu_custom_call" | custom-call | flops 56000000000 | bytes 62914560 | tf_op jit(solution)/shard_map/feed/pallas_call | solution.py:497
  248.0 23.1 %fc_grads.1 = bf16[4,768,1536]{2,1,0:T(8,128)(2,1)} custom-call(bf16[1568,768]{1,0:T(8,128)(2,1)} %bitcast.63, bf16[1568,768]{1,0:T(8,128)(2,1)} %bitcast.47, bf16[4,1568,768]{2,1,0:T(8,128)(2,1)} %bitcast.49, bf16[4,1568,768]{2,1,0:T(8,128)(2,1)} %bitcast.48), custom_call_target="tpu_custom_call" | custom-call | flops 14797504512 | bytes 19267584 | tf_op jit(solution)/shard_map/fc_grads/pallas_call | solution.py:628
  271.2 20.7 %spatial_bwd.2 = (bf16[1,784,768]{2,1,0:T(8,128)(2,1)}, bf16[1,784,768]{2,1,0:T(8,128)(2,1)}, bf16[1,784,768]{2,1,0:T(8,128)(2,1)}) custom-call(s32[1]{0:T(128)S(6)} %copy.56.width_ref, bf16[1,784,2304]{2,1,0:T(8,128)(2,1)} %bitcast.59, bf16[1,784,2304]{2,1,0:T(8,128)(2,1)} %bitcast.60, bf16[1,784,2304]{2,1,0:T(8,128)(2,1)} %bitcast.61, ...), custom_call_target="tpu_custom_call" | custom-call | flops 32000000000 | bytes 9437184 | tf_op jit(solution)/shard_map/spatial_bwd/pallas_call | solution.py:175
  291.9 12.8 %middle_bwd.2 = (f32[784,768]{1,0:T(8,128)}, bf16[784,768]{1,0:T(8,128)(2,1)}, bf16[4,208,768]{2,1,0:T(8,128)(2,1)}, f32[8,768]{1,0:T(8,128)}) custom-call(bf16[784,768]{1,0:T(8,128)(2,1)} %bitcast.64, bf16[784,768]{1,0:T(8,128)(2,1)} %bitcast.66, bf16[784,768]{1,0:T(8,128)(2,1)} %bitcast.68, bf16[768,2304]{1,0:T(8,128)(2,1)} %w_ref.9, ...), custom_call_target="tpu_custom_call" | custom-call | flops 14000000000 | bytes 16777216 | tf_op jit(solution)/shard_map/middle_bwd/pallas_call | solution.py:537
  304.6 3.5 all-to-all-start.2
  308.2 21.0 %spatial_bwd.3 = (bf16[1,784,768]{2,1,0:T(8,128)(2,1)}, bf16[1,784,768]{2,1,0:T(8,128)(2,1)}, bf16[1,784,768]{2,1,0:T(8,128)(2,1)}) custom-call(s32[1]{0:T(128)S(6)} %copy.56.width_ref, bf16[1,784,2304]{2,1,0:T(8,128)(2,1)} %bitcast.53, bf16[1,784,2304]{2,1,0:T(8,128)(2,1)} %bitcast.54, bf16[1,784,2304]{2,1,0:T(8,128)(2,1)} %bitcast.55, ...), custom_call_target="tpu_custom_call" | custom-call | flops 32000000000 | bytes 9437184 | tf_op jit(solution)/shard_map/spatial_bwd/pallas_call | solution.py:175
  329.2 9.3 %all-to-all-done.2.refs_0_ = bf16[4,208,768]{2,1,0:T(8,128)(2,1)S(1)} async-done(((bf16[4,208,768]{2,1,0:T(8,128)(2,1)}), bf16[4,208,768]{2,1,0:T(8,128)(2,1)S(1)}, u32[]{:S(2)}, u32[]{:S(2)}) %all-to-all-start.2) | async-done | bytes 1277984 | tf_op jit(solution)/shard_map/all_to_all | solution.py:1261
  338.6 13.1 %middle_bwd.3 = (f32[784,768]{1,0:T(8,128)}, bf16[784,768]{1,0:T(8,128)(2,1)}, bf16[4,208,768]{2,1,0:T(8,128)(2,1)}, f32[8,768]{1,0:T(8,128)}) custom-call(bf16[784,768]{1,0:T(8,128)(2,1)} %bitcast.70, bf16[784,768]{1,0:T(8,128)(2,1)} %bitcast.72, bf16[784,768]{1,0:T(8,128)(2,1)} %bitcast.74, bf16[768,2304]{1,0:T(8,128)(2,1)} %w_ref.9, ...), custom_call_target="tpu_custom_call" | custom-call | flops 14000000000 | bytes 16777216 | tf_op jit(solution)/shard_map/middle_bwd/pallas_call | solution.py:537
  351.7 3.7 all-to-all-start.3
  355.6 6.0 %weight_grad.7.refs_9_ = bf16[768,768]{1,0:T(8,128)(2,1)} custom-call(bf16[784,768]{1,0:T(8,128)(2,1)} %get-tuple-element.115.refs_0_, bf16[784,768]{1,0:T(8,128)(2,1)} %get-tuple-element.116.refs_1_, bf16[784,768]{1,0:T(8,128)(2,1)} %bitcast.69, bf16[784,768]{1,0:T(8,128)(2,1)} %bitcast.75), custom_call_target="tpu_custom_call" | custom-call | flops 1849688064 | bytes 4816896 | tf_op jit(solution)/shard_map/weight_grad/pallas_call | solution.py:602
  361.6 6.1 %weight_grad.6.refs_8_ = bf16[768,768]{1,0:T(8,128)(2,1)} custom-call(bf16[784,768]{1,0:T(8,128)(2,1)} %get-tuple-element.115.refs_0_, bf16[784,768]{1,0:T(8,128)(2,1)} %get-tuple-element.116.refs_1_, bf16[784,768]{1,0:T(8,128)(2,1)} %bitcast.67, bf16[784,768]{1,0:T(8,128)(2,1)} %bitcast.73), custom_call_target="tpu_custom_call" | custom-call | flops 1849688064 | bytes 4816896 | tf_op jit(solution)/shard_map/weight_grad/pallas_call | solution.py:602
  367.6 6.0 %weight_grad.8.refs_10_ = bf16[768,768]{1,0:T(8,128)(2,1)} custom-call(bf16[784,768]{1,0:T(8,128)(2,1)} %bitcast.41, bf16[784,768]{1,0:T(8,128)(2,1)} %bitcast.43, bf16[1568,768]{1,0:T(8,128)(2,1)} %bitcast.32, bf16[1568,768]{1,0:T(8,128)(2,1)} %bitcast.33), custom_call_target="tpu_custom_call" | custom-call | flops 1849688064 | bytes 4816896 | tf_op jit(solution)/shard_map/weight_grad/pallas_call | solution.py:602
  373.7 6.0 %weight_grad.5.refs_7_ = bf16[768,768]{1,0:T(8,128)(2,1)} custom-call(bf16[784,768]{1,0:T(8,128)(2,1)} %get-tuple-element.115.refs_0_, bf16[784,768]{1,0:T(8,128)(2,1)} %get-tuple-element.116.refs_1_, bf16[784,768]{1,0:T(8,128)(2,1)} %bitcast.65, bf16[784,768]{1,0:T(8,128)(2,1)} %bitcast.71), custom_call_target="tpu_custom_call" | custom-call | flops 1849688064 | bytes 4816896 | tf_op jit(solution)/shard_map/weight_grad/pallas_call | solution.py:602
  379.6 6.3 %weight_grad.9.refs_11_ = bf16[768,768]{1,0:T(8,128)(2,1)} custom-call(bf16[4,208,768]{2,1,0:T(8,128)(2,1)} %copy-done, bf16[4,208,768]{2,1,0:T(8,128)(2,1)} %copy-done.1, bf16[784,768]{1,0:T(8,128)(2,1)} %get-tuple-element.118.refs_2_, bf16[784,768]{1,0:T(8,128)(2,1)} %get-tuple-element.119.refs_3_), custom_call_target="tpu_custom_call" | custom-call | flops 1849688064 | bytes 4816896 | tf_op jit(solution)/shard_map/weight_grad/pallas_call | solution.py:602
  386.7 1.0 copy-done.3
  387.8 148.6 %temporal_tail.1 = (bf16[4,2,208,768]{3,2,1,0:T(8,128)(2,1)}, bf16[8,768,768]{2,1,0:T(8,128)(2,1)}, f32[24,768]{1,0:T(8,128)}) custom-call(f32[768]{0:T(1024)} %gain_ref.15, f32[768]{0:T(1024)} %shift_ref.9, f32[24,768]{1,0:T(8,128)} %maximum_maximum_fusion.small_in, bf16[4,208,768]{2,1,0:T(8,128)(2,1)} %copy-done.2, bf16[4,208,768]{2,1,0:T(8,128)(2,1)} %copy-done.3, ...), custom_call_target="tpu_custom_call" | custom-call | flops 23555211264 | bytes 62914560 | tf_op jit(solution)/shard_map/temporal_tail/pallas_call | solution.py:1065
  537.7 10.3 %finish.1 = (f32[768,2304]{1,0:T(8,128)}, f32[768,2304]{1,0:T(8,128)}, f32[768,768]{1,0:T(8,128)}, f32[768,768]{1,0:T(8,128)}) custom-call(bf16[8,768,768]{2,1,0:T(8,128)(2,1)} %get-tuple-element.128.time_ref.space_ref.space_proj_ref.time_proj_ref, bf16[8,768,768]{2,1,0:T(8,128)(2,1)} %get-tuple-element.128.time_ref.space_ref.space_proj_ref.time_proj_ref, ...), custom_call_target="tpu_custom_call" | custom-call | flops 1000000000 | bytes 31457280 | tf_op jit(solution)/shard_map/finish/pallas_call | solution.py:660
  549.4 8.1 %norm_out.1 = f32[2,784,768]{2,1,0:T(8,128)} custom-call(bf16[4,2,208,768]{3,2,1,0:T(8,128)(2,1)} %get-tuple-element.120.grad_ref, bf16[2,784,768]{2,1,0:T(8,128)(2,1)} %bitcast.39, f32[768]{0:T(1024)} %gain_ref.15, f32[784,768]{1,0:T(8,128)} %get-tuple-element.121.refs_0_, f32[784,768]{1,0:T(8,128)} %get-tuple-element.126.refs_1_), custom_call_target="tpu_custom_call" | custom-call | flops 1000000000 | bytes 26214400 | tf_op jit(solution)/shard_map/norm_out/pallas_call | solution.py:571
  557.5 1.0 bitcast_convert_fusion
  (54 shorter events, 6.6 us)
Async XLA Ops:
  7.2 1.7 copy-start.12
  7.2 1.8 copy-start.4
  7.2 94.2 %all-gather.6.cloned.1.call-start = ((), (), s32[]{:S(2)}) async-start(), calls=%async_computation.9 | async-start | bytes 1720320 | tf_op jit(solution)/shard_map/all_gather | solution.py:1265
  9.0 0.9 copy-start.9
  9.8 186.5 %all-gather.4.cloned.1.call-start = ((), (), s32[]{:S(2)}) async-start(), calls=%async_computation.6 | async-start | bytes 10616832 | tf_op jit(solution)/shard_map/all_gather | solution.py:1275
  103.8 6.5 %copy-start.10 = (f32[1536]{0:T(1024)S(1)}, f32[1536]{0:T(1024)}, u32[]{:S(2)}) copy-start(f32[1536]{0:T(1024)} %param.32) | copy-start | bytes 18436
  103.8 35.8 %all-to-all-start = ((bf16[4,208,768]{2,1,0:T(8,128)(2,1)}), bf16[4,208,768]{2,1,0:T(8,128)(2,1)S(1)}, u32[]{:S(2)}, u32[]{:S(2)}) async-start(bf16[4,208,768]{2,1,0:T(8,128)(2,1)} %get-tuple-element.80), calls=%async_computation | async-start | bytes 2555904 | tf_op jit(solution)/shard_map/all_to_all | solution.py:1261
  139.7 3.6 copy-start
  139.7 33.6 %all-to-all-start.1 = ((bf16[4,208,768]{2,1,0:T(8,128)(2,1)}), bf16[4,208,768]{2,1,0:T(8,128)(2,1)S(1)}, u32[]{:S(2)}, u32[]{:S(2)}) async-start(bf16[4,208,768]{2,1,0:T(8,128)(2,1)} %get-tuple-element.82), calls=%async_computation.1 | async-start | bytes 2555904 | tf_op jit(solution)/shard_map/all_to_all | solution.py:1261
  143.2 243.5 %reduce-scatter.3.cloned.1.call-start = ((), (), s32[]{:S(2)}) async-start(), calls=%async_computation.7 | async-start | bytes 10616832 | tf_op jit(solution)/shard_map/reduce_scatter | solution.py:1296
  173.3 1.0 copy-start.1
  304.6 33.9 %all-to-all-start.2 = ((bf16[4,208,768]{2,1,0:T(8,128)(2,1)}), bf16[4,208,768]{2,1,0:T(8,128)(2,1)S(1)}, u32[]{:S(2)}, u32[]{:S(2)}) async-start(bf16[4,208,768]{2,1,0:T(8,128)(2,1)} %get-tuple-element.101), calls=%async_computation.2 | async-start | bytes 2555904 | tf_op jit(solution)/shard_map/all_to_all | solution.py:1261
  338.6 13.1 %copy-start.2 = (bf16[4,208,768]{2,1,0:T(8,128)(2,1)}, bf16[4,208,768]{2,1,0:T(8,128)(2,1)S(1)}, u32[]{:S(2)}) copy-start(bf16[4,208,768]{2,1,0:T(8,128)(2,1)S(1)} %all-to-all-done.2.refs_0_) | copy-start | bytes 3833860
  351.7 3.8 copy-start.5
  351.7 3.9 copy-start.11
  351.7 35.0 %all-to-all-start.3 = ((bf16[4,208,768]{2,1,0:T(8,128)(2,1)}), bf16[4,208,768]{2,1,0:T(8,128)(2,1)S(1)}, u32[]{:S(2)}, u32[]{:S(2)}) async-start(bf16[4,208,768]{2,1,0:T(8,128)(2,1)} %get-tuple-element.110), calls=%async_computation.3 | async-start | bytes 2555904 | tf_op jit(solution)/shard_map/all_to_all | solution.py:1261
  355.4 202.1 %reduce-scatter.5.cloned.1.call-start = ((), (), s32[]{:S(2)}) async-start(), calls=%async_computation.8 | async-start | bytes 1474560 | tf_op jit(solution)/shard_map/reduce_scatter | solution.py:1321
  379.6 6.3 %copy-start.7 = (f32[8,768]{1,0:T(8,128)S(1)}, f32[8,768]{1,0:T(8,128)}, u32[]{:S(2)}) copy-start(f32[8,768]{1,0:T(8,128)} %get-tuple-element.99) | copy-start | bytes 73732
  379.6 6.3 %copy-start.8 = (f32[8,768]{1,0:T(8,128)S(1)}, f32[8,768]{1,0:T(8,128)}, u32[]{:S(2)}) copy-start(f32[8,768]{1,0:T(8,128)} %get-tuple-element.108) | copy-start | bytes 73732
  386.7 1.0 copy-start.3
  537.7 10.4 %copy-start.6 = (f32[24,768]{1,0:T(8,128)S(1)}, f32[24,768]{1,0:T(8,128)}, u32[]{:S(2)}) copy-start(f32[24,768]{1,0:T(8,128)} %get-tuple-element.127) | copy-start | bytes 221188
Sparse Core Ops, SparseCore 0:
  10.2 64.8 all-gather.5
  103.9 61.6 all-gather.3
  271.3 80.7 reduce-scatter.2
  386.8 47.7 reduce-scatter.4
